TPU v7x, 32 devices: a whole 2x2x4 slice. The times are simulated.
32 devices in a mesh: pack: 4 (over y, x), blk: 4 (over z), head: 2 (over core).
Axes of the slice: x: 2, y: 2, z: 4, core: 2. Of those that a mesh axis runs over, the one named last changes fastest.
Arguments:
- tokens_full: bfloat16 [4, 3072, 1152], P('pack', 'blk'), may hold values from -6 to 6
- condition: bfloat16 [4, 9, 1152], P('pack'), may hold values from -6 to 6
- kept_index: int32 [4, 1536], P('pack', 'blk'), may hold values from 0 to 3071, as said below
- segment_ids: int32 [4, 1536], P('pack'), may hold values from 0 to 8, as said below
- cotangent: bfloat16 [4, 3072, 1152], P('pack', 'blk'), may hold values from -6 to 6
- qkv_weight: bfloat16 [1152, 3, 1152], P(None, None, 'head'), may hold values from -0.1875 to 0.1875
- query_value_bias: bfloat16 [2, 1152], P(None, 'head'), may hold values from -3 to 3
- output_weight: bfloat16 [1152, 1152], P('head'), may hold values from -2 to 2
- output_bias: bfloat16 [1152], replicated, may hold values from -2 to 2
- hidden_weight: bfloat16 [1152, 4608], P(None, 'head'), may hold values from -0.1875 to 0.1875
- hidden_bias: bfloat16 [4608], P('head'), may hold values from -2 to 2
- down_weight: bfloat16 [4608, 1152], P('head'), may hold values from -0.09375 to 0.09375
- down_bias: bfloat16 [1152], replicated, may hold values from -2 to 2
- modulation_weight: bfloat16 [1152, 6, 1152], P(None, None, 'head'), may hold values from -0.1875 to 0.1875
- modulation_bias: bfloat16 [6, 1152], P(None, 'head'), may hold values from -2 to 2
Outputs:
- block_output: bfloat16 [4, 3072, 1152], P('pack', 'blk')
- tokens_grad: bfloat16 [4, 3072, 1152], P('pack', 'blk')
- condition_grad: float32 [4, 9, 1152], P('pack')
- qkv_weight_grad: float32 [1152, 3, 1152], P('blk', None, 'head')
- query_value_bias_grad: float32 [2, 1152], P(None, 'head')
- output_weight_grad: float32 [1152, 1152], P('head', 'blk')
- output_bias_grad: float32 [1152], replicated
- hidden_weight_grad: float32 [1152, 4608], P('blk', 'head')
- hidden_bias_grad: float32 [4608], P('head')
- down_weight_grad: float32 [4608, 1152], P('head', 'blk')
- down_bias_grad: float32 [1152], replicated
- modulation_weight_grad: float32 [1152, 6, 1152], P('blk', None, 'head')
- modulation_bias_grad: float32 [6, 1152], P(None, 'head')
Inputs may be any that keep to these rules, and one draw needn't show every extreme that they name: `kept_index`: within a pack, the kept tokens j * 384 to (j + 1) * 384 - 1 hold distinct positions from 2 * j * 384 to 2 * (j + 1) * 384 - 1; the first block keeps position 0 and the last keeps the pack's last position. `segment_ids`: each pack is 1 latents of 512 kept tokens and the others of 128, in an order drawn per pack; the ids never fall along a pack, and each id from 0 to 8 names one latent.
All inputs are finite; a program needn't handle non-finite values.
Results may differ from a plain program's by a relative error of at most 0.015.
The roundings to bfloat16 on the way count: a program that leaves them out, or rounds other values in their place, can miss the bound.
Values may be sent and summed in bfloat16 or wider, within the bound.
No kernel may reach another device: no remote copies, remote signals or barrier semaphores. Data moves between devices by JAX's collectives and lax.ppermute only.
A program may use at most 320 MiB of HBM per device.

v0:
```python
from functools import partial
import math

import jax
import jax.numpy as jnp
from jax import lax
from jax.sharding import PartitionSpec as P

HEAD_DIM = 72


EPSILON = 1e-06
MASKED = -1e30
HIGHEST = lax.Precision.HIGHEST


def with_halo(block, sides, width):
    for axis, dim in sides:
        count = lax.axis_size(axis)
        forward = [(i, i + 1) for i in range(count - 1)]
        backward = [(target, source) for source, target in forward]
        low = lax.ppermute(
            lax.slice_in_dim(block, block.shape[dim] - width, None, axis=dim), axis, forward
        )
        high = lax.ppermute(lax.slice_in_dim(block, 0, width, axis=dim), axis, backward)
        block = jnp.concatenate([low, block, high], axis=dim)
    return block


def layer_norm(values):
    center = values - jnp.mean(values, axis=-1, keepdims=True)
    spread = jnp.mean(center * center, axis=-1, keepdims=True)
    inverse = lax.rsqrt(spread + EPSILON)
    return (center * inverse, inverse)


def norm_back(upstream, normed, inverse):
    mean_grad = jnp.mean(upstream, axis=-1, keepdims=True)
    mean_cross = jnp.mean(upstream * normed, axis=-1, keepdims=True)
    return inverse * (upstream - mean_grad - normed * mean_cross)


def split_heads(matrix):
    return matrix.reshape(matrix.shape[0], -1, HEAD_DIM).transpose(1, 0, 2)


def join_heads(stacked):
    return stacked.transpose(1, 0, 2).reshape(stacked.shape[1], -1)


def bf_dot(operand_a, operand_b):
    return jnp.dot(operand_a, operand_b, preferred_element_type=jnp.float32)


def turn_rows(matrix, axis_dim, blocks, groups):
    shape_now = matrix.shape
    pieces = shape_now[axis_dim] // (blocks * groups)
    spread_shape = shape_now[:axis_dim] + (blocks, groups, pieces) + shape_now[axis_dim + 1 :]
    return jnp.swapaxes(matrix.reshape(spread_shape), axis_dim, axis_dim + 1).reshape(shape_now)


def local(
    tokens_full,
    condition,
    kept_index,
    segment_ids,
    cotangent,
    qkv_weight,
    query_value_bias,
    output_weight,
    output_bias,
    hidden_weight,
    hidden_bias,
    down_weight,
    down_bias,
    modulation_weight,
    modulation_bias,
):
    model_width = tokens_full.shape[2]
    local_width = qkv_weight.shape[2]
    own_tokens = kept_index.shape[1]
    seg_count = condition.shape[1]
    factor = 1.0 / math.sqrt(HEAD_DIM)
    cycle_place = lax.axis_index("blk")
    local_index = kept_index[0] - cycle_place * (2 * own_tokens)
    full_rows = tokens_full[0]
    kept_rows = jnp.take(full_rows, local_index, axis=0).astype(jnp.float32)
    segments = segment_ids[0]
    own_segments = lax.dynamic_slice_in_dim(segments, cycle_place * own_tokens, own_tokens, 0)
    outside = jnp.full((own_tokens,), -1, jnp.int32)
    padded_segments = jnp.concatenate([outside, segments, outside])
    near_segments = lax.dynamic_slice_in_dim(
        padded_segments, cycle_place * own_tokens, 3 * own_tokens, 0
    )
    one_hot = (own_segments[:, None] == jnp.arange(seg_count, dtype=jnp.int32)[None, :]).astype(
        jnp.float32
    )
    same_doc = own_segments[:, None] == near_segments[None, :]
    cond_rows = condition[0].astype(jnp.float32)
    active = jax.nn.silu(cond_rows).astype(jnp.bfloat16)
    mod_own = (
        jnp.einsum("sd,dgf->sgf", active, modulation_weight, preferred_element_type=jnp.float32)
        + modulation_bias.astype(jnp.float32)[None]
    )
    mod_all = lax.all_gather(mod_own, "head", axis=2, tiled=True)
    per_token = jnp.dot(one_hot, mod_all.reshape(seg_count, 6 * model_width), precision=HIGHEST)
    pieces = [
        per_token[:, number * model_width : (number + 1) * model_width] for number in range(6)
    ]
    shift_one, scale_one, gate_one, shift_two, scale_two, gate_two = pieces
    normed_one, inverse_one = layer_norm(kept_rows)
    hidden_one = (normed_one * (1.0 + scale_one) + shift_one).astype(jnp.bfloat16)
    flat_qkv = qkv_weight.reshape(model_width, 3 * local_width)
    projected = bf_dot(hidden_one, flat_qkv)
    bias_rows = query_value_bias.astype(jnp.float32)
    queries = (projected[:, :local_width] + bias_rows[0]).astype(jnp.bfloat16)
    key_rows = projected[:, local_width : 2 * local_width].astype(jnp.bfloat16)
    value_rows = (projected[:, 2 * local_width :] + bias_rows[1]).astype(jnp.bfloat16)
    kv_pair = jnp.concatenate([key_rows, value_rows], axis=1)
    near_pair = with_halo(kv_pair, (("blk", 0),), own_tokens)
    near_keys = near_pair[:, :local_width]
    near_values = near_pair[:, local_width:]

    def head_forward(operands):
        query_head, key_head, value_head = operands
        scores = bf_dot(query_head, key_head.T) * factor
        scores = jnp.where(same_doc, scores, MASKED)
        row_peak = jnp.max(scores, axis=1, keepdims=True)
        exponent = jnp.exp(scores - row_peak)
        row_total = jnp.sum(exponent, axis=1, keepdims=True)
        weights = (exponent / row_total).astype(jnp.bfloat16)
        return (bf_dot(weights, value_head), row_peak[:, 0] + jnp.log(row_total[:, 0]))

    head_out, log_total = lax.map(
        head_forward, (split_heads(queries), split_heads(near_keys), split_heads(near_values))
    )
    attended = join_heads(head_out).astype(jnp.bfloat16)
    branch_one = lax.psum(bf_dot(attended, output_weight), "head") + output_bias.astype(jnp.float32)
    middle = kept_rows + gate_one * branch_one
    normed_two, inverse_two = layer_norm(middle)
    hidden_two = (normed_two * (1.0 + scale_two) + shift_two).astype(jnp.bfloat16)
    pre_act = bf_dot(hidden_two, hidden_weight) + hidden_bias.astype(jnp.float32)
    gelu_out = jax.nn.gelu(pre_act, approximate=True).astype(jnp.bfloat16)
    branch_two = lax.psum(bf_dot(gelu_out, down_weight).astype(jnp.bfloat16), "head").astype(
        jnp.float32
    ) + down_bias.astype(jnp.float32)
    result_rows = middle + gate_two * branch_two
    block_output = full_rows.at[local_index].set(result_rows.astype(jnp.bfloat16))[None]
    cot_rows = cotangent[0]
    upstream = jnp.take(cot_rows, local_index, axis=0).astype(jnp.float32)
    down_in = (gate_two * upstream).astype(jnp.bfloat16)
    down_weight_grad = bf_dot(gelu_out.T, down_in)
    down_bias_grad = jnp.sum(down_in.astype(jnp.float32), axis=0)
    gelu_grad = bf_dot(down_in, down_weight.T)
    pre_grad = jax.vjp(partial(jax.nn.gelu, approximate=True), pre_act)[1](gelu_grad)[0].astype(
        jnp.bfloat16
    )
    hidden_weight_grad = bf_dot(hidden_two.T, pre_grad)
    hidden_bias_grad = jnp.sum(pre_grad.astype(jnp.float32), axis=0)
    hidden_two_grad = lax.psum(bf_dot(pre_grad, hidden_weight.T), "head")
    middle_grad = upstream + norm_back(hidden_two_grad * (1.0 + scale_two), normed_two, inverse_two)
    branch_grad = (gate_one * middle_grad).astype(jnp.bfloat16)
    output_weight_grad = bf_dot(attended.T, branch_grad)
    output_bias_grad = jnp.sum(branch_grad.astype(jnp.float32), axis=0)
    attended_grad = bf_dot(branch_grad, output_weight.T).astype(jnp.bfloat16)

    def head_backward(operands):
        query_head, key_head, value_head, grad_head, log_head = operands
        scores = bf_dot(query_head, key_head.T) * factor
        scores = jnp.where(same_doc, scores, MASKED)
        weights = jnp.exp(scores - log_head[:, None])
        weight_grad = bf_dot(grad_head, value_head.T)
        row_dot = jnp.sum(weights * weight_grad, axis=1, keepdims=True)
        score_grad = (weights * (weight_grad - row_dot)).astype(jnp.bfloat16)
        query_grad = bf_dot(score_grad, key_head) * factor
        key_grad = bf_dot(score_grad.T, query_head) * factor
        value_grad = bf_dot(weights.astype(jnp.bfloat16).T, grad_head)
        return (query_grad, key_grad, value_grad)

    query_grads, key_grads, value_grads = lax.map(
        head_backward,
        (
            split_heads(queries),
            split_heads(near_keys),
            split_heads(near_values),
            split_heads(attended_grad),
            log_total,
        ),
    )
    kv_term = jnp.concatenate([join_heads(key_grads), join_heads(value_grads)], axis=1)
    lower_term = kv_term[:own_tokens]
    own_term = kv_term[own_tokens : 2 * own_tokens]
    upper_term = kv_term[2 * own_tokens :]
    returned = with_halo(
        jnp.concatenate([lower_term, upper_term], axis=0).astype(jnp.bfloat16),
        (("blk", 0),),
        own_tokens,
    ).astype(jnp.float32)
    kv_share = own_term + returned[:own_tokens] + returned[3 * own_tokens :]
    qkv_grad = jnp.concatenate(
        [join_heads(query_grads).astype(jnp.bfloat16), kv_share.astype(jnp.bfloat16)], axis=1
    )
    qkv_weight_grad = bf_dot(hidden_one.T, qkv_grad).reshape(model_width, 3, local_width)
    column_sums = jnp.sum(qkv_grad.astype(jnp.float32), axis=0)
    query_value_bias_grad = jnp.stack([column_sums[:local_width], column_sums[2 * local_width :]])
    hidden_one_grad = lax.psum(bf_dot(qkv_grad, flat_qkv.T).astype(jnp.bfloat16), "head").astype(
        jnp.float32
    )
    input_grad = middle_grad + norm_back(
        hidden_one_grad * (1.0 + scale_one), normed_one, inverse_one
    )
    tokens_grad = cot_rows.at[local_index].set(input_grad.astype(jnp.bfloat16))[None]
    token_mod_grad = jnp.concatenate(
        [
            hidden_one_grad,
            hidden_one_grad * normed_one,
            middle_grad * branch_one,
            hidden_two_grad,
            hidden_two_grad * normed_two,
            upstream * branch_two,
        ],
        axis=1,
    )
    mod_grad = jnp.dot(one_hot.T, token_mod_grad, precision=HIGHEST).reshape(
        seg_count, 6, model_width
    )
    own_mod_grad = lax.dynamic_slice_in_dim(
        mod_grad, lax.axis_index("head") * local_width, local_width, 2
    )
    modulation_bias_grad = jnp.sum(own_mod_grad, axis=0)
    cond_term = jnp.einsum(
        "sgf,dgf->sd", own_mod_grad, modulation_weight.astype(jnp.float32), precision=HIGHEST
    )
    cond_total = lax.psum(cond_term.astype(jnp.bfloat16), ("blk", "head")).astype(jnp.float32)
    squashed = jax.nn.sigmoid(cond_rows)
    condition_grad = (cond_total * squashed * (1.0 + cond_rows * (1.0 - squashed)))[None]
    active_wide = active.astype(jnp.float32)
    blocks = lax.axis_size("blk")
    groups = lax.axis_size("pack")
    mod_term = jnp.einsum("sd,sgf->dgf", active_wide, own_mod_grad, precision=HIGHEST)
    spread_out = (
        lax.psum_scatter(
            turn_rows(qkv_weight_grad, 0, blocks, groups),
            ("pack", "blk"),
            scatter_dimension=0,
            tiled=True,
        ),
        lax.psum_scatter(
            turn_rows(output_weight_grad, 1, blocks, groups),
            ("pack", "blk"),
            scatter_dimension=1,
            tiled=True,
        ),
        lax.psum_scatter(
            turn_rows(hidden_weight_grad, 0, blocks, groups),
            ("pack", "blk"),
            scatter_dimension=0,
            tiled=True,
        ),
        lax.psum_scatter(
            turn_rows(down_weight_grad, 1, blocks, groups),
            ("pack", "blk"),
            scatter_dimension=1,
            tiled=True,
        ),
        lax.psum_scatter(
            turn_rows(mod_term, 0, blocks, groups), ("pack", "blk"), scatter_dimension=0, tiled=True
        ),
    )
    totals = (
        lax.all_gather(spread_out[0].astype(jnp.bfloat16), "pack", axis=0, tiled=True).astype(
            jnp.float32
        ),
        lax.all_gather(spread_out[1].astype(jnp.bfloat16), "pack", axis=1, tiled=True).astype(
            jnp.float32
        ),
        lax.all_gather(spread_out[2].astype(jnp.bfloat16), "pack", axis=0, tiled=True).astype(
            jnp.float32
        ),
        lax.all_gather(spread_out[3].astype(jnp.bfloat16), "pack", axis=1, tiled=True).astype(
            jnp.float32
        ),
        lax.all_gather(spread_out[4].astype(jnp.bfloat16), "pack", axis=0, tiled=True).astype(
            jnp.float32
        ),
    )
    modulation_weight_grad = totals[4]
    bias_totals = lax.psum(
        (
            query_value_bias_grad,
            output_bias_grad,
            hidden_bias_grad,
            down_bias_grad,
            modulation_bias_grad,
        ),
        ("pack", "blk"),
    )
    return (
        block_output,
        tokens_grad,
        condition_grad,
        totals[0],
        bias_totals[0],
        totals[1],
        bias_totals[1],
        totals[2],
        bias_totals[2],
        totals[3],
        bias_totals[3],
        modulation_weight_grad,
        bias_totals[4],
    )


def solution(mesh):
    in_specs = (
        P("pack", "blk", None),
        P("pack", None, None),
        P("pack", "blk"),
        P("pack", None),
        P("pack", "blk", None),
        P(None, None, "head"),
        P(None, "head"),
        P("head", None),
        P(),
        P(None, "head"),
        P("head"),
        P("head", None),
        P(),
        P(None, None, "head"),
        P(None, "head"),
    )
    out_specs = (
        P("pack", "blk", None),
        P("pack", "blk", None),
        P("pack", None, None),
        P("blk", None, "head"),
        P(None, "head"),
        P("head", "blk"),
        P(),
        P("blk", "head"),
        P("head"),
        P("head", "blk"),
        P(),
        P("blk", None, "head"),
        P(None, "head"),
    )
    return jax.shard_map(local, mesh=mesh, in_specs=in_specs, out_specs=out_specs, check_vma=False)
```

profile of v0, /device:TPU:0, one launch (start us, length us, event | category | flops | bytes accessed | tf_op | source)
XLA Modules:
  0.0 1439.2 jit_solution(10884803392295747105)
XLA Ops:
  7.3 3.0 copy.139
  11.6 5.3 gather_fusion
  20.1 5.6 convolution_add_fusion.1
  25.7 2.2 copy.68
  27.9 24.6 %all_gather.18 = f32[9,6,1152]{0,1,2:T(8,128)} all-gather(f32[9,6,576]{0,1,2:T(8,128)} %copy.68), channel_id=1, replica_groups=mesh['pack'=4,'blk'=4,'head'=2] {'head'}, dimensions={2}, use_global_device_ids=true | all-gather | bytes 373248 | tf_op jit(solution)/shard_map/all_gather | solution.py:105
  52.4 3.4 copy.69
  56.6 4.3 fusion.90
  61.6 4.5 copy-done.64
  66.2 2.4 fusion.119
  72.7 6.4 collective-permute-start
  79.7 2.2 copy.70
  82.7 13.9 collective-permute-done.1
  97.7 4.5 pad_maximum_fusion.1
  103.9 3.8 copy.71
  107.7 3.8 copy.72
  111.6 39.1 %while.28 = (s32[]{:T(128)}, bf16[8,384,72]{1,2,0:T(8,128)(2,1)S(1)}, f32[8,384]{1,0:T(8,128)}, bf16[8,384,72]{2,1,0:T(8,128)(2,1)}, bf16[8,1152,72]{2,1,0:T(8,1...) while((s32[]{:T(128)}, ...), condition=%wide.region_5.7_spmd.clone, body=%wide.region_2.0_spmd.clone.sunk | while | flops 131382912 | bytes 6134897 | solution.py:134
  153.6 2.8 gather_fusion.1
  156.3 20.6 %all-reduce.7.cloned.1.call-done = f32[384,1152]{1,0:T(8,128)} async-done(((f32[384,1152]{1,0:T(8,128)}), f32[384,1152]{1,0:T(8,128)}) %all-reduce.7.cloned.1.call-update) | async-done | bytes 1769488 | tf_op jit(solution)/shard_map/psum | solution.py:138
  176.9 4.4 convert_reduce_fusion.3
  181.7 2.6 fusion.74
  184.3 5.3 fusion.121
  189.7 6.2 convert_reduce_fusion
  197.1 3.7 fusion.122
  201.2 21.7 %all-reduce.9.cloned.1.call-done = f32[384,1152]{1,0:T(8,128)} async-done(((f32[384,1152]{1,0:T(8,128)}), f32[384,1152]{1,0:T(8,128)}) %all-reduce.9.cloned.1.call-update) | async-done | bytes 1769488 | tf_op jit(solution)/shard_map/psum | solution.py:160
  222.9 2.7 fusion.109
  225.6 4.0 convert_reduce_fusion.4
  231.8 76.1 %while.29 = (s32[]{:T(128)}, bf16[8,384,72]{1,2,0:T(8,128)(2,1)S(1)}, f32[8,1152,72]{1,2,0:T(8,128)}, f32[8,1152,72]{1,2,0:T(8,128)}, bf16[8,384,72]{2,1,0:T(8,1...) while((s32[]{:T(128)}, ...), condition=%wide.region_16.18_spmd.clone, body=%wide.region_14.17_spmd.clone.sunk | while | flops 323038848 | bytes 15342209 | solution.py:180
  308.0 2.8 fusion.45
  311.0 4.0 collective-permute-start.2
  316.3 6.7 convolution_convert_fusion.1
  323.0 11.3 collective-permute-done.2
  334.3 4.2 collective-permute-done.3
  338.8 2.9 convolution_convert_fusion
  343.0 5.1 fusion.110
  348.0 4.9 copy.80
  354.1 4.4 fusion.123
  358.5 5.0 copy.79
  365.7 3.1 fusion.88
  372.8 3.6 fusion.89
  378.9 5.5 fusion.53
  384.4 29.9 %psum.74 = bf16[9,1152]{1,0:T(8,128)(2,1)S(1)} all-reduce(bf16[9,1152]{1,0:T(8,128)(2,1)S(1)} %fusion.53), channel_id=1, replica_groups=mesh['pack'=4,'blk'=4,'head'=2] {'blk','head'}, use_global_device_ids=true, to_apply=%region_21.23 | all-reduce | flops 10368 | bytes 41472 | tf_op jit(solution)/shard_map/psum | solution.py:234
  415.1 7.1 convolution_bitcast_fusion.2
  422.2 6.6 copy.82
  428.9 2.3 copy.77
  431.2 2.3 convolution_bitcast_fusion.4
  435.6 7.0 fusion.86
  442.6 14.2 reshape_reshape.3
  456.8 8.8 copy.76
  465.6 88.5 %reduce-scatter.12.cloned.1.call-done = f32[2304,72]{0,1:T(8,128)} async-done(((f32[2304,1152]{0,1:T(8,128)}), f32[2304,72]{0,1:T(8,128)}) %reduce-scatter.12.cloned.1.call-update) | async-done | bytes 663568 | tf_op jit(solution)/shard_map/reduce_scatter | solution.py:260
  556.1 185.3 %reduce-scatter.10.cloned.1.call-done = f32[72,2304]{1,0:T(8,128)} async-done(((f32[1152,2304]{1,0:T(8,128)}), f32[72,2304]{1,0:T(8,128)}) %reduce-scatter.10.cloned.1.call-update) | async-done | bytes 663568 | tf_op jit(solution)/shard_map/reduce_scatter | solution.py:254
  743.3 275.4 %reduce-scatter.14.cloned.1.call-done = f32[72,6,576]{2,0,1:T(8,128)} async-done(((f32[1152,6,576]{2,0,1:T(8,128)}), f32[72,6,576]{2,0,1:T(8,128)}) %reduce-scatter.14.cloned.1.call-update) | async-done | bytes 995344 | tf_op jit(solution)/shard_map/reduce_scatter | solution.py:266
  1022.4 6.3 scatter_custom_fusion
  1029.5 7.4 scatter_custom_fusion.1
  1036.9 76.9 %all-reduce.1 = (f32[2,576]{1,0:T(2,128)}, f32[1152]{0:T(1024)}, f32[2304]{0:T(1024)}, f32[1152]{0:T(1024)}, f32[6,576]{1,0:T(8,128)}) all-reduce(f32[2,576]{1,0:T(2,128)S(1)} %pad_maximum_fusion.9, f32[1152]{0:T(1024)S(1)} %copy-done.48, f32[2304]{0:T(1024)S(1)} %copy-done.53, ...), channel_id=1, replica_groups=mesh['pack'=4,'blk'=4,'head'=2] {'pack','blk'}, use_global_device_ids=true, to_apply=%region_24.26 | all-reduce | flops 9216 | bytes 73728 | tf_op jit(solution)/shard_map/psum | solution.py:288
  1113.8 41.3 %reduce-scatter.16.cloned.1.call-done = f32[576,72]{0,1:T(8,128)} async-done(((f32[576,1152]{0,1:T(8,128)}), f32[576,72]{0,1:T(8,128)}) %reduce-scatter.16.cloned.1.call-update) | async-done | bytes 165904
  1156.0 9.8 all_gather.20
  1166.7 161.6 %reduce-scatter.8.cloned.1.call-done = f32[72,3,576]{2,0,1:T(8,128)} async-done(((f32[1152,3,576]{2,0,1:T(8,128)}), f32[72,3,576]{2,0,1:T(8,128)}) %reduce-scatter.8.cloned.1.call-update) | async-done | bytes 497680 | tf_op jit(solution)/shard_map/reduce_scatter | solution.py:242
  1329.4 16.5 %all_gather.19 = bf16[288,3,576]{2,0,1:T(8,128)(2,1)S(1)} all-gather(bf16[72,3,576]{2,0,1:T(8,128)(2,1)S(1)} %convert_element_type.198), channel_id=1, replica_groups=mesh['pack'=4,'blk'=4,'head'=2] {'pack'}, dimensions={0}, use_global_device_ids=true | all-gather | bytes 1244160 | tf_op jit(solution)/shard_map/all_gather | solution.py:271
  1347.4 11.9 all-gather.6.cloned.1.call-done
  1359.3 3.0 convert_element_type.208
  1362.2 27.8 %all-gather.4.cloned.1.call-done = bf16[288,2304]{1,0:T(8,128)(2,1)} async-done(((bf16[72,2304]{1,0:T(8,128)(2,1)}), bf16[288,2304]{1,0:T(8,128)(2,1)}) %all-gather.4.cloned.1.call-update) | async-done | bytes 1327120 | tf_op jit(solution)/shard_map/all_gather | solution.py:277
  1390.1 3.1 convert_element_type.205
  1393.2 35.2 %all-gather.8.cloned.1.call-done = bf16[288,6,576]{2,0,1:T(8,128)(2,1)} async-done(((bf16[72,6,576]{2,0,1:T(8,128)(2,1)}), bf16[288,6,576]{2,0,1:T(8,128)(2,1)}) %all-gather.8.cloned.1.call-update) | async-done | bytes 1990672 | tf_op jit(solution)/shard_map/all_gather | solution.py:283
  1428.4 4.0 convert_element_type.211
  (332 shorter events, 164.5 us)
Async XLA Ops:
  7.2 143.5 %copy-start = (bf16[576,1152]{1,0:T(8,128)(2,1)S(1)}, bf16[576,1152]{1,0:T(8,128)(2,1)}, u32[]{:S(2)}) copy-start(bf16[576,1152]{1,0:T(8,128)(2,1)} %param.28) | copy-start | bytes 3981316
  7.2 169.7 %all-reduce.7.cloned.1.call-start = ((), (), s32[]{:S(2)}) async-start(), calls=%async_computation.5 | async-start | bytes 3538944 | tf_op jit(solution)/shard_map/psum | solution.py:138
  7.2 3.0 copy-start.28
  10.4 143.2 %copy-start.3 = (bf16[1,768,1152]{2,1,0:T(8,128)(2,1)}, bf16[1,768,1152]{2,1,0:T(8,128)(2,1)S(1)}, u32[]{:S(2)}) copy-start(bf16[1,768,1152]{2,1,0:T(8,128)(2,1)S(1)} %copy.140) | copy-start | bytes 5308420
  10.9 50.1 %copy-start.40 = (pred[384]{0:T(512)(128)(4,1)}, pred[384]{0:T(512)(128)(4,1)S(1)}, u32[]{:S(2)}) copy-start(pred[384]{0:T(512)(128)(4,1)S(1)} %compare_and_fusion) | copy-start | bytes 1156
  11.0 6.0 copy-start.49
  16.9 3.1 copy-start.30
  18.5 42.5 %copy-start.35 = (f32[384]{0:T(512)}, f32[384]{0:T(512)S(1)}, u32[]{:S(2)}) copy-start(f32[384]{0:T(512)S(1)} %broadcast_multiply_fusion.5) | copy-start | bytes 4612
  20.1 40.9 %copy-start.44 = (f32[384]{0:T(512)}, f32[384]{0:T(512)S(1)}, u32[]{:S(2)}) copy-start(f32[384]{0:T(512)S(1)} %add_rsqrt_fusion.1) | copy-start | bytes 4612
  56.6 4.4 copy-start.4
  61.0 7.6 copy-start.2
  61.0 5.1 copy-start.64
  61.6 7.0 copy-start.16
  66.2 2.5 copy-start.51
  66.2 2.5 copy-start.52
  69.7 9.4 copy-start.55
  71.4 25.1 %collective-permute-start.1 = (bf16[384,1152]{0,1:T(8,128)(2,1)}, bf16[384,1152]{0,1:T(8,128)(2,1)}, u32[]{:S(2)}, u32[]{:S(2)}) collective-permute-start(bf16[384,1152]{0,1:T(8,128)(2,1)} %pad_maximum_fusion.6), channel_id=1, source_target_pairs={{2,0},{4,2},{6,4},{3,1},{5,3},{7,5},{10,8},{12,10},{14,12},{11,9},... | collective-permute-start | bytes 2654216 | tf_op jit(solution)/shard_map/ppermute | solution.py:25
  72.7 25.0 %collective-permute-start = (bf16[384,1152]{0,1:T(8,128)(2,1)}, bf16[384,1152]{0,1:T(8,128)(2,1)}, u32[]{:S(2)}, u32[]{:S(2)}) collective-permute-start(bf16[384,1152]{0,1:T(8,128)(2,1)} %pad_maximum_fusion.6), channel_id=1, source_target_pairs={{0,2},{2,4},{4,6},{1,3},{3,5},{5,7},{8,10},{10,12},{12,14},{9,11},... | collective-permute-start | bytes 2654216 | tf_op jit(solution)/shard_map/ppermute | solution.py:22
  150.7 2.1 copy-start.26
  152.9 70.0 %all-reduce.9.cloned.1.call-start = ((), (), s32[]{:S(2)}) async-start(), calls=%async_computation.6 | async-start | bytes 3538944 | tf_op jit(solution)/shard_map/psum | solution.py:160
  153.5 23.4 %copy-start.33 = (f32[1152]{0:T(1024)}, f32[1152]{0:T(1024)S(1)}, u32[]{:S(2)}) copy-start(f32[1152]{0:T(1024)S(1)} %convert_element_type.175) | copy-start | bytes 13828
  153.6 23.4 %copy-start.41 = (pred[384]{0:T(512)(128)(4,1)S(1)}, pred[384]{0:T(512)(128)(4,1)}, u32[]{:S(2)}) copy-start(pred[384]{0:T(512)(128)(4,1)} %copy-done.40) | copy-start | bytes 1156
  181.3 2.9 copy-start.23
  181.7 44.0 %copy-start.38 = (f32[384]{0:T(512)}, f32[384]{0:T(512)S(1)}, u32[]{:S(2)}) copy-start(f32[384]{0:T(512)S(1)} %add_rsqrt_fusion) | copy-start | bytes 4612
  181.7 8.0 slice-start
  184.2 5.4 copy-start.17
  184.3 5.4 slice-start.1
  200.8 163.3 %all-reduce.11.cloned.1.call-start = ((), (), s32[]{:S(2)}) async-start(), calls=%async_computation.15 | async-start | bytes 3538944 | tf_op jit(solution)/shard_map/psum | solution.py:144
  222.9 2.7 copy-start.6
  222.9 2.8 copy-start.9
  310.8 5.5 copy-start.19
  311.0 23.3 %collective-permute-start.2 = (bf16[384,1152]{0,1:T(8,128)(2,1)S(1)}, bf16[384,1152]{0,1:T(8,128)(2,1)S(1)}, u32[]{:S(2)}, u32[]{:S(2)}) collective-permute-start(bf16[384,1152]{0,1:T(8,128)(2,1)S(1)} %get-tuple-element.277), channel_id=1, source_target_pairs={{0,2},{2,4},{4,6},{1,3},{3,5},{5,7},{8,10},{10,12},{12,14},{9,11},... | collective-permute-start | bytes 2654216 | tf_op jit(solution)/shard_map/ppermute | solution.py:22
  314.9 23.5 %collective-permute-start.3 = (bf16[384,1152]{0,1:T(8,128)(2,1)S(1)}, bf16[384,1152]{0,1:T(8,128)(2,1)S(1)}, u32[]{:S(2)}, u32[]{:S(2)}) collective-permute-start(bf16[384,1152]{0,1:T(8,128)(2,1)S(1)} %get-tuple-element.278), channel_id=1, source_target_pairs={{2,0},{4,2},{6,4},{3,1},{5,3},{7,5},{10,8},{12,10},{14,12},{11,9},... | collective-permute-start | bytes 2654216 | tf_op jit(solution)/shard_map/ppermute | solution.py:25
  316.3 22.2 %copy-start.11 = (f32[8,1152,72]{1,2,0:T(8,128)S(1)}, f32[8,1152,72]{1,2,0:T(8,128)}, u32[]{:S(2)}) copy-start(f32[8,1152,72]{1,2,0:T(8,128)} %get-tuple-element.110) | copy-start | bytes 7962628
  316.3 22.2 %copy-start.12 = (f32[8,1152,72]{1,2,0:T(8,128)S(1)}, f32[8,1152,72]{1,2,0:T(8,128)}, u32[]{:S(2)}) copy-start(f32[8,1152,72]{1,2,0:T(8,128)} %get-tuple-element.109) | copy-start | bytes 7962628
  323.0 15.9 %copy-start.65 = (bf16[1152,3,576]{0,2,1:T(8,128)(2,1)S(1)}, bf16[1152,3,576]{0,2,1:T(8,128)(2,1)}, u32[]{:S(2)}) copy-start(bf16[1152,3,576]{0,2,1:T(8,128)(2,1)} %param.26) | copy-start | bytes 11943940
  338.8 3.0 copy-start.13
  341.8 212.3 %reduce-scatter.12.cloned.1.call-start = ((), (), s32[]{:S(2)}) async-start(), calls=%async_computation.10 | async-start | bytes 11280384 | tf_op jit(solution)/shard_map/reduce_scatter | solution.py:260
  352.9 388.4 %reduce-scatter.10.cloned.1.call-start = ((), (), s32[]{:S(2)}) async-start(), calls=%async_computation.8 | async-start | bytes 11280384 | tf_op jit(solution)/shard_map/reduce_scatter | solution.py:254
  363.5 2.0 copy-start.5
  363.5 2.0 copy-start.36
  363.6 655.0 %reduce-scatter.14.cloned.1.call-start = ((), (), s32[]{:S(2)}) async-start(), calls=%async_computation.12 | async-start | bytes 18800640 | tf_op jit(solution)/shard_map/reduce_scatter | solution.py:266
  365.7 3.2 copy-start.8
  365.7 3.2 copy-start.15
  365.7 3.2 copy-start.34
  378.9 35.4 %copy-start.31 = (bf16[1,9,1152]{2,1,0:T(8,128)(2,1)S(1)}, bf16[1,9,1152]{2,1,0:T(8,128)(2,1)}, u32[]{:S(2)}) copy-start(bf16[1,9,1152]{2,1,0:T(8,128)(2,1)} %param.22) | copy-start | bytes 62212
  428.8 2.3 copy-start.27
  428.8 726.2 %reduce-scatter.16.cloned.1.call-start = ((), (), s32[]{:S(2)}) async-start(), calls=%async_computation.14 | async-start | bytes 3133440
  435.3 893.1 %reduce-scatter.8.cloned.1.call-start = ((), (), s32[]{:S(2)}) async-start(), calls=%async_computation.7 | async-start | bytes 9400320 | tf_op jit(solution)/shard_map/reduce_scatter | solution.py:242
  465.6 893.7 %all-gather.6.cloned.1.call-start = ((), (), s32[]{:S(2)}) async-start(), calls=%async_computation.11 | async-start | bytes 1658880 | tf_op jit(solution)/shard_map/all_gather | solution.py:280
  556.0 464.7 %copy-start.60 = (s32[1,384]{1,0:T(1,128)S(1)}, s32[1,384]{1,0:T(1,128)}, u32[]{:S(2)}) copy-start(s32[1,384]{1,0:T(1,128)} %param.23) | copy-start | bytes 4612
  556.0 834.1 %all-gather.4.cloned.1.call-start = ((), (), s32[]{:S(2)}) async-start(), calls=%async_computation.9 | async-start | bytes 1658880 | tf_op jit(solution)/shard_map/all_gather | solution.py:277
  743.2 685.2 %all-gather.8.cloned.1.call-start = ((), (), s32[]{:S(2)}) async-start(), calls=%async_computation.13 | async-start | bytes 2764800 | tf_op jit(solution)/shard_map/all_gather | solution.py:283
  1022.3 6.4 copy-start.29
  1022.3 7.0 copy-start.57
  1022.3 7.0 copy-start.56
  1022.4 7.0 copy-start.37
  1022.4 7.0 copy-start.43
  1022.4 7.0 copy-start.46
  1029.4 7.5 copy-start.32
  1029.4 7.5 copy-start.47
  1029.4 7.5 copy-start.48
  1029.4 7.5 copy-start.53
  1390.1 42.3 %copy-start.1 = (bf16[576,1152]{1,0:T(8,128)(2,1)S(1)}, bf16[576,1152]{1,0:T(8,128)(2,1)}, u32[]{:S(2)}) copy-start(bf16[576,1152]{1,0:T(8,128)(2,1)} %param.28) | copy-start | bytes 3981316
  (19 other events, 21.3 us)
Sparse Core Ops, SparseCore 0:
  153.0 23.8 all-reduce.6
  201.0 21.8 all-reduce.8
  341.9 20.6 all-reduce.10
  369.3 184.7 reduce-scatter.11
  559.8 181.4 reduce-scatter.9
  748.2 270.3 reduce-scatter.13
  1025.0 130.0 reduce-scatter.15
  1161.7 166.5 reduce-scatter.7
  1330.9 28.3 all-gather.5
  1361.1 28.9 all-gather.3
  1392.1 36.2 all-gather.7
where the time goes:
time: 1450 us; the launch traced here: 1440 us
  waiting for transfers between devices  900 us (62%)
  matrix products  168 us (12%)
  blocking collectives  158 us (11%)
  local copies, waits for them, and re-layouts  106 us (7%)
  other arithmetic  77.3 us (5%)
  between operations  15.1 us (1%)
  starting transfers between devices  14.7 us (1%)
    reduce_scatter x1, waiting for transfers between devices, local(): lax.psum_scatter(turn_rows(mod_term, 0, blocks, groups), ('pack', 'blk'),...  275 us
    reduce_scatter x1, waiting for transfers between devices, local(): lax.psum_scatter(turn_rows(hidden_weight_grad, 0, blocks, groups), ('pack...  185 us
    reduce_scatter x1, waiting for transfers between devices, local(): lax.psum_scatter(turn_rows(qkv_weight_grad, 0, blocks, groups), ('pack',...  162 us
    dot_general x68, matrix products, bf_dot(): return jnp.dot(operand_a, operand_b, preferred_element_type=jnp.float32)  142 us
    reduce_scatter x1, waiting for transfers between devices, local(): lax.psum_scatter(turn_rows(down_weight_grad, 1, blocks, groups), ('pack',...  88.5 us
    psum x1, blocking collectives, local(): lax.psum((query_value_bias_grad, output_bias_grad, hidden_bias_grad, down...  76.9 us
    unnamed x12, waiting for transfers between devices  41.4 us
    all_gather x1, waiting for transfers between devices, local(): lax.all_gather(spread_out[4].astype(jnp.bfloat16), 'pack', axis=0, tiled=...  35.2 us
  transfers between devices with their start and end apart: 15, of which 14 were waited for; matrix products, arithmetic and copies ran while one was open for 9% of the time, Pallas kernels for 0%

commit v1 on v0

v1 whole, which is shorter than its diff:
```python
import math

import jax
import jax.numpy as jnp
from jax import lax
from jax.sharding import PartitionSpec as P

HEAD_DIM = 72
SHORT = 128
LANES = 128
EPSILON = 1e-06
MASKED = -1e30


def bf_dot(operand_a, operand_b):
    return jnp.dot(operand_a, operand_b, preferred_element_type=jnp.float32)


def exact_rows(picker, rows):
    high = rows.astype(jnp.bfloat16)
    low = (rows - high.astype(jnp.float32)).astype(jnp.bfloat16)
    return bf_dot(picker, high) + bf_dot(picker, low)


def layer_norm(values):
    center = values - jnp.mean(values, axis=-1, keepdims=True)
    spread = jnp.mean(center * center, axis=-1, keepdims=True)
    inverse = lax.rsqrt(spread + EPSILON)
    return (center * inverse, inverse)


def norm_back(upstream, normed, inverse):
    mean_grad = jnp.mean(upstream, axis=-1, keepdims=True)
    mean_cross = jnp.mean(upstream * normed, axis=-1, keepdims=True)
    return inverse * (upstream - mean_grad - normed * mean_cross)


def xor_permute(block, axis, bits):
    return lax.ppermute(block, axis, [(i, i ^ bits) for i in range(lax.axis_size(axis))])


def swap(block):
    return xor_permute(block, "head", 1)


def head_sum(block):
    return block.astype(jnp.float32) + swap(block).astype(jnp.float32)


def move(block, step):
    count = lax.axis_size("blk")
    pairs = [(i, i + step) for i in range(count) if 0 <= i + step < count]
    return lax.ppermute(block, "blk", pairs)


def axis_bits(axis, turned):
    bits = [1 << b for b in range((lax.axis_size(axis) - 1).bit_length())]
    return bits[::-1] if turned else bits


def gather_xor(block, axis, turned=False):
    held = {0: block}
    for bits in axis_bits(axis, turned):
        for entry in list(held):
            held[entry ^ bits] = xor_permute(held[entry], axis, bits)
    return [held[entry] for entry in range(lax.axis_size(axis))]


def in_order(entries, axis):
    order = jnp.arange(len(entries), dtype=jnp.int32) ^ lax.axis_index(axis)
    return jnp.take(jnp.stack(entries), order, axis=0)


def windows(width, parts):
    tiles = width // LANES
    size = -(-tiles // parts)
    return [LANES * (q * (tiles - size) // (parts - 1)) for q in range(parts)], size * LANES


def trade_columns(block, axis):
    count = lax.axis_size(axis)
    starts, size = windows(block.shape[1], count)
    table = jnp.asarray(starts, jnp.int32)
    me = lax.axis_index(axis)
    out = []
    for entry in range(count):
        piece = lax.dynamic_slice_in_dim(block, table[me ^ entry], size, 1)
        out.append(xor_permute(piece, axis, entry) if entry else piece)
    return out


def trade_pieces(pieces, axis):
    me = lax.axis_index(axis)
    out = []
    for entry in range(lax.axis_size(axis)):
        piece = lax.dynamic_index_in_dim(pieces, me ^ entry, 0, keepdims=False)
        out.append(xor_permute(piece, axis, entry) if entry else piece)
    return out


def gather_rows(block, turned):
    width = block.shape[1]
    half = -(-width // (2 * LANES)) * LANES
    core = lax.axis_index("head")
    own = jnp.where(core == 0, block[:, :half], block[:, width - half :])
    own = jnp.concatenate(gather_xor(own, "pack", turned), axis=0)
    other = swap(own)
    low = jnp.where(core == 0, own, other)
    high = jnp.where(core == 0, other, own)
    return jnp.concatenate([low, high[:, 2 * half - width :]], axis=1)


def sum_blk(term):
    count = lax.axis_size("blk")
    me = lax.axis_index("blk")
    rows = term.shape[0] // count
    total = lax.dynamic_slice_in_dim(term, me * rows, rows, 0)
    for step in range(1, count):
        target = lax.rem(me + step, count)
        piece = lax.dynamic_slice_in_dim(term, target * rows, rows, 0).astype(jnp.bfloat16)
        pairs = [(i, (i + step) % count) for i in range(count)]
        total = total + lax.ppermute(piece, "blk", pairs).astype(jnp.float32)
    return total


def weight_grad(rows, columns, turned):
    term = lax.dot_general(
        rows,
        jnp.concatenate(columns, axis=0),
        (((0,), (0,)), ((), ())),
        preferred_element_type=jnp.float32,
    )
    share = sum_blk(term).astype(jnp.bfloat16)
    return in_order(gather_xor(share, "pack", turned), "pack")


def join_windows(stacked, width):
    starts, size = windows(width, stacked.shape[0])
    parts = []
    for q, start in enumerate(starts):
        end = starts[q + 1] if q + 1 < len(starts) else width
        parts.append(stacked[q, :, : end - start])
    return jnp.concatenate(parts, axis=1).astype(jnp.float32)


def split_heads(matrix):
    return matrix.reshape(matrix.shape[0], -1, HEAD_DIM).transpose(1, 0, 2)


def join_heads(stacked):
    return stacked.transpose(1, 0, 2).reshape(stacked.shape[1], -1)


def local(
    tokens_full,
    condition,
    kept_index,
    segment_ids,
    cotangent,
    qkv_weight,
    query_value_bias,
    output_weight,
    output_bias,
    hidden_weight,
    hidden_bias,
    down_weight,
    down_bias,
    modulation_weight,
    modulation_bias,
):
    width = tokens_full.shape[2]
    own_width = qkv_weight.shape[2]
    hidden = hidden_weight.shape[1]
    count = kept_index.shape[1]
    seg_count = condition.shape[1]
    places = count // SHORT
    longs = (segment_ids.shape[1] - SHORT * seg_count) // (3 * SHORT)
    packs = lax.axis_size("pack")
    blocks = lax.axis_size("blk")
    factor = 1.0 / math.sqrt(HEAD_DIM)
    blk = lax.axis_index("blk")
    core = lax.axis_index("head")

    local_index = kept_index[0] - blk * (2 * count)
    full_rows = tokens_full[0]
    cot_rows = cotangent[0]
    picker = (
        local_index[:, None] == jnp.arange(full_rows.shape[0], dtype=jnp.int32)[None, :]
    ).astype(jnp.bfloat16)
    kept_low = bf_dot(picker, full_rows).astype(jnp.bfloat16)
    kept_rows = kept_low.astype(jnp.float32)
    upstream = bf_dot(picker, cot_rows)

    segments = segment_ids[0]
    outside = jnp.full((count,), -1, jnp.int32)
    padded = jnp.concatenate([outside, segments, outside])
    near = lax.dynamic_slice_in_dim(padded, blk * count, 3 * count, 0)
    own_segments = near[count : 2 * count]
    reaches_low = near[count - 1] == near[count]

    def beside(block):
        low, high = move(block, 1), move(block, -1)
        if longs == 1:
            return jnp.where(reaches_low, low, high)
        return jnp.concatenate([low, high], axis=0)

    if longs == 1:
        beside_segments = jnp.where(reaches_low, near[:count], near[2 * count :])
    else:
        beside_segments = jnp.concatenate([near[:count], near[2 * count :]])
    all_segments = jnp.concatenate([own_segments, beside_segments])
    half = count // 2
    own_half = lax.dynamic_slice_in_dim(kept_low, core * half, half, 0)
    near_half = beside(own_half)
    other_half = swap(near_half)
    first = jnp.where(core == 0, near_half, other_half).reshape(-1, half, width)
    second = jnp.where(core == 0, other_half, near_half).reshape(-1, half, width)
    near_rows = jnp.concatenate([first, second], axis=1).reshape(-1, width).astype(jnp.float32)

    cond_rows = condition[0].astype(jnp.float32)
    active = jax.nn.silu(cond_rows).astype(jnp.bfloat16)
    mod_own = (
        jnp.einsum("sd,dgf->sgf", active, modulation_weight, preferred_element_type=jnp.float32)
        + modulation_bias.astype(jnp.float32)[None]
    )
    mod_other = swap(mod_own)
    mod_all = jnp.concatenate(
        [jnp.where(core == 0, mod_own, mod_other), jnp.where(core == 0, mod_other, mod_own)],
        axis=2,
    )
    place_segments = jnp.maximum(all_segments[::SHORT], 0)
    mod_places = jnp.take(mod_all, place_segments, axis=0)

    def per_token(number, first, last):
        picked = mod_places[first:last, number]
        return jnp.broadcast_to(picked[:, None], (last - first, SHORT, width)).reshape(-1, width)

    shift_one, scale_one, gate_one, shift_two, scale_two, gate_two = [
        per_token(number, 0, places) for number in range(6)
    ]
    down_in = (gate_two * upstream).astype(jnp.bfloat16)
    down_in_all = gather_rows(down_in, False)

    normed_one, inverse_one = layer_norm(kept_rows)
    hidden_one = (normed_one * (1.0 + scale_one) + shift_one).astype(jnp.bfloat16)
    hidden_one_all = gather_rows(hidden_one, True)
    near_hidden = (
        layer_norm(near_rows)[0] * (1.0 + per_token(1, places, mod_places.shape[0]))
        + per_token(0, places, mod_places.shape[0])
    ).astype(jnp.bfloat16)

    flat_qkv = qkv_weight.reshape(width, 3 * own_width)
    bias_rows = query_value_bias.astype(jnp.float32)
    projected = bf_dot(jnp.concatenate([hidden_one, near_hidden], axis=0), flat_qkv)
    queries = (projected[:, :own_width] + bias_rows[0]).astype(jnp.bfloat16)
    key_rows = projected[:, own_width : 2 * own_width].astype(jnp.bfloat16)
    value_rows = (projected[:, 2 * own_width :] + bias_rows[1]).astype(jnp.bfloat16)
    head_rows = (split_heads(queries), split_heads(key_rows), split_heads(value_rows))
    same_doc = all_segments[:, None] == all_segments[None, :]

    def probs_of(query_head, key_head, mask):
        scores = jnp.where(mask, bf_dot(query_head, key_head.T) * factor, MASKED)
        exponent = jnp.exp(scores - jnp.max(scores, axis=1, keepdims=True))
        return exponent / jnp.sum(exponent, axis=1, keepdims=True)

    def head_forward(operands):
        query_head, key_head, value_head = operands
        probs = probs_of(query_head[:count], key_head, same_doc[:count])
        return bf_dot(probs.astype(jnp.bfloat16), value_head)

    attended = join_heads(lax.map(head_forward, head_rows)).astype(jnp.bfloat16)
    packs_width = own_width // packs
    attended_split = attended.reshape(count, packs, packs_width).transpose(1, 0, 2)
    attended_all = trade_pieces(attended_split, "pack")

    branch_one = head_sum(bf_dot(attended, output_weight)) + output_bias.astype(jnp.float32)
    middle = kept_rows + gate_one * branch_one
    normed_two, inverse_two = layer_norm(middle)
    hidden_two = (normed_two * (1.0 + scale_two) + shift_two).astype(jnp.bfloat16)
    hidden_two_all = gather_rows(hidden_two, False)
    pre_act = bf_dot(hidden_two, hidden_weight) + hidden_bias.astype(jnp.float32)
    gelu_out, gelu_back = jax.vjp(lambda v: jax.nn.gelu(v, approximate=True), pre_act)
    gelu_out = gelu_out.astype(jnp.bfloat16)
    gelu_all = trade_columns(gelu_out, "pack")
    gelu_grad = bf_dot(down_in, down_weight.T)
    pre_grad = gelu_back(gelu_grad)[0].astype(jnp.bfloat16)
    pre_all = trade_columns(pre_grad, "pack")
    hidden_two_grad = head_sum(bf_dot(pre_grad, hidden_weight.T))
    branch_two = head_sum(bf_dot(gelu_out, down_weight).astype(jnp.bfloat16))
    branch_two = branch_two + down_bias.astype(jnp.float32)
    result_rows = middle + gate_two * branch_two

    def put_rows(base, rows):
        spread = lax.dot_general(
            picker, rows, (((0,), (0,)), ((), ())), preferred_element_type=jnp.float32
        )
        kept = jnp.max(picker, axis=0)[:, None] > 0
        return jnp.where(kept, spread.astype(jnp.bfloat16), base)[None]

    block_output = put_rows(full_rows, result_rows.astype(jnp.bfloat16))

    middle_grad = upstream + norm_back(hidden_two_grad * (1.0 + scale_two), normed_two, inverse_two)
    branch_grad = (gate_one * middle_grad).astype(jnp.bfloat16)
    attended_grad = bf_dot(branch_grad, output_weight.T).astype(jnp.bfloat16)
    near_grad = beside(attended_grad)
    branch_grad_all = gather_rows(branch_grad, True)

    def head_backward(operands):
        query_head, key_head, value_head, grad_head = operands
        probs = probs_of(query_head, key_head, same_doc)
        weight_grad_ = bf_dot(grad_head, value_head.T)
        row_dot = jnp.sum(probs * weight_grad_, axis=1, keepdims=True)
        score_grad = (probs * (weight_grad_ - row_dot)).astype(jnp.bfloat16)
        query_grad = bf_dot(score_grad[:count], key_head) * factor
        key_grad = bf_dot(score_grad[:, :count].T, query_head) * factor
        value_grad = bf_dot(probs[:, :count].astype(jnp.bfloat16).T, grad_head)
        return (query_grad, key_grad, value_grad)

    grads = lax.map(
        head_backward,
        (*head_rows, split_heads(jnp.concatenate([attended_grad, near_grad], axis=0))),
    )
    grads = [join_heads(grad).astype(jnp.bfloat16) for grad in grads]
    qkv_grad = jnp.concatenate(grads, axis=1)
    qkv_split = (
        jnp.stack(grads, axis=1)
        .reshape(count, 3, packs, packs_width)
        .transpose(2, 0, 1, 3)
        .reshape(packs, count, 3 * packs_width)
    )
    qkv_all = trade_pieces(qkv_split, "pack")
    hidden_one_grad = head_sum(bf_dot(qkv_grad, flat_qkv.T).astype(jnp.bfloat16))
    input_grad = middle_grad + norm_back(
        hidden_one_grad * (1.0 + scale_one), normed_one, inverse_one
    )
    tokens_grad = put_rows(cot_rows, input_grad.astype(jnp.bfloat16))

    down_stack = weight_grad(down_in_all, gelu_all, False)
    down_weight_grad = join_windows(down_stack, hidden).T
    hidden_stack = weight_grad(hidden_two_all, pre_all, True)
    hidden_weight_grad = join_windows(hidden_stack, hidden)
    output_stack = weight_grad(branch_grad_all, attended_all, False)
    output_weight_grad = (
        output_stack.transpose(0, 2, 1).reshape(own_width, -1).astype(jnp.float32)
    )
    qkv_stack = weight_grad(hidden_one_all, qkv_all, True)
    qkv_weight_grad = (
        qkv_stack.reshape(packs, -1, 3, packs_width)
        .transpose(1, 2, 0, 3)
        .reshape(-1, 3, own_width)
        .astype(jnp.float32)
    )

    terms = jnp.stack(
        [
            hidden_one_grad,
            hidden_one_grad * normed_one,
            middle_grad * branch_one,
            hidden_two_grad,
            hidden_two_grad * normed_two,
            upstream * branch_two,
        ],
        axis=1,
    )
    place_sums = jnp.sum(terms.reshape(places, SHORT, 6, width), axis=1)
    own_sums = lax.dynamic_slice_in_dim(place_sums, core * own_width, own_width, 2)
    grad_sums = jnp.sum(qkv_grad.astype(jnp.float32), axis=0)
    bias_terms = (
        grad_sums[:own_width],
        grad_sums[2 * own_width :],
        jnp.sum(branch_grad.astype(jnp.float32), axis=0),
        jnp.sum(pre_grad.astype(jnp.float32), axis=0),
        jnp.sum(down_in.astype(jnp.float32), axis=0),
    )
    place_active = jnp.take(active, place_segments[:places], axis=0).astype(jnp.float32)
    sent = jnp.concatenate([own_sums.reshape(-1), place_active.reshape(-1), *bias_terms])
    sent = sent.reshape(-1, LANES)
    by_blk = in_order(gather_xor(sent, "blk"), "blk")
    by_pack = in_order(gather_xor(by_blk, "pack"), "pack")
    received = by_pack.reshape(packs * blocks, -1)
    cut = places * 6 * own_width
    sums_all = received[:, :cut].reshape(-1, 6 * own_width)
    active_all = received[:, cut : cut + places * width].reshape(-1, width)
    biases = jnp.sum(received[:, cut + places * width :], axis=0)
    modulation_bias_grad = jnp.sum(sums_all, axis=0).reshape(6, own_width)
    rows = width // blocks
    active_share = lax.dynamic_slice_in_dim(active_all, blk * rows, rows, 1)
    sums_high = sums_all.astype(jnp.bfloat16)
    sums_low = (sums_all - sums_high.astype(jnp.float32)).astype(jnp.bfloat16)
    active_share = active_share.astype(jnp.bfloat16).T
    modulation_weight_grad = (
        bf_dot(active_share, sums_high) + bf_dot(active_share, sums_low)
    ).reshape(rows, 6, own_width)

    pack_sums = lax.dynamic_index_in_dim(
        sums_all.reshape(packs, -1, 6 * own_width), lax.axis_index("pack"), 0, keepdims=False
    )
    of_segment = (
        jnp.arange(seg_count, dtype=jnp.int32)[:, None] == segments[None, ::SHORT]
    ).astype(jnp.bfloat16)
    mod_grad = exact_rows(of_segment, pack_sums)
    mod_high = mod_grad.astype(jnp.bfloat16)
    mod_low = (mod_grad - mod_high.astype(jnp.float32)).astype(jnp.bfloat16)
    cond_terms = jnp.einsum(
        "sgf,dgf->sd",
        jnp.concatenate([mod_high, mod_low], axis=0).reshape(-1, 6, own_width),
        modulation_weight,
        preferred_element_type=jnp.float32,
    )
    cond_total = head_sum(cond_terms[:seg_count] + cond_terms[seg_count:])
    squashed = jax.nn.sigmoid(cond_rows)
    condition_grad = (cond_total * squashed * (1.0 + cond_rows * (1.0 - squashed)))[None]

    ends = [own_width, 2 * own_width, 2 * own_width + width, 2 * own_width + width + hidden]
    value_bias = jnp.stack([biases[: ends[0]], biases[ends[0] : ends[1]]])
    return (
        block_output,
        tokens_grad,
        condition_grad,
        qkv_weight_grad,
        value_bias,
        output_weight_grad,
        biases[ends[1] : ends[2]],
        hidden_weight_grad,
        biases[ends[2] : ends[3]],
        down_weight_grad,
        biases[ends[3] :],
        modulation_weight_grad,
        modulation_bias_grad,
    )


def solution(mesh):
    in_specs = (
        P("pack", "blk", None),
        P("pack", None, None),
        P("pack", "blk"),
        P("pack", None),
        P("pack", "blk", None),
        P(None, None, "head"),
        P(None, "head"),
        P("head", None),
        P(),
        P(None, "head"),
        P("head"),
        P("head", None),
        P(),
        P(None, None, "head"),
        P(None, "head"),
    )
    out_specs = (
        P("pack", "blk", None),
        P("pack", "blk", None),
        P("pack", None, None),
        P("blk", None, "head"),
        P(None, "head"),
        P("head", "blk"),
        P(),
        P("blk", "head"),
        P("head"),
        P("head", "blk"),
        P(),
        P("blk", None, "head"),
        P(None, "head"),
    )
    return jax.shard_map(local, mesh=mesh, in_specs=in_specs, out_specs=out_specs, check_vma=False)
```

time: 1450 us -> 575 us (0.40)
  waiting for transfers between devices: 900 us -> 158 us
  blocking collectives: 158 us -> 0 us
  starting transfers between devices: 14.7 us -> 93.4 us
  local copies, waits for them, and re-layouts: 106 us -> 72.2 us
  matrix products: 168 us -> 151 us
    reduce_scatter x4 -> x0, waiting for transfers between devices: 711 us -> none  [the longest x1 275 us: local(): lax.psum_scatter(turn_rows(mod_term, 0, blocks, groups), ('pack', 'blk'),...]
    ppermute x4 -> x69, waiting for transfers between devices: 30.5 us -> 158 us  [the longest x53 123 us: xor_permute(): lax.ppermute(block, axis, [(i, i ^ bits) for i in range(lax.axis_size(axi...]
    psum x2 -> x0, blocking collectives: 107 us -> none  [the longest x1 76.9 us: local(): lax.psum((query_value_bias_grad, output_bias_grad, hidden_bias_grad, down...]
    ppermute x4 -> x69, starting transfers between devices: 12.9 us -> 93.4 us  [the longest x53 52.2 us: xor_permute(): lax.ppermute(block, axis, [(i, i ^ bits) for i in range(lax.axis_size(axi...]
    all_gather x3 -> x0, waiting for transfers between devices: 74.9 us -> none  [the longest x1 35.2 us: local(): lax.all_gather(spread_out[4].astype(jnp.bfloat16), 'pack', axis=0, tiled=...]
    all_gather x3 -> x0, blocking collectives: 50.8 us -> none  [the longest x1 24.6 us: local(): mod_all = lax.all_gather(mod_own, 'head', axis=2, tiled=True)]
    psum x3 -> x0, waiting for transfers between devices: 42.3 us -> none  [the longest x1 21.7 us: local(): hidden_two_grad = lax.psum(bf_dot(pre_grad, hidden_weight.T), 'head')]
    unnamed x12 -> x0, waiting for transfers between devices: 41.4 us -> none
  transfers between devices with their start and end apart: 15 -> 69, of which waited for: 14 -> 31; matrix products, arithmetic and copies ran while one was open for 9% -> 50% of each run, Pallas kernels for 0% -> 0%
where the time goes in v1:
time: 575 us; the launch traced here: 564 us
  waiting for transfers between devices  158 us (27%)
  matrix products  151 us (26%)
  starting transfers between devices  93.4 us (16%)
  other arithmetic  76.8 us (13%)
  local copies, waits for them, and re-layouts  72.2 us (13%)
  between operations  11.8 us (2%)
    dot_general x70, matrix products, bf_dot(): return jnp.dot(operand_a, operand_b, preferred_element_type=jnp.float32)  125 us
    ppermute x53, waiting for transfers between devices, xor_permute(): lax.ppermute(block, axis, [(i, i ^ bits) for i in range(lax.axis_size(axi...  123 us
    ppermute x53, starting transfers between devices, xor_permute(): lax.ppermute(block, axis, [(i, i ^ bits) for i in range(lax.axis_size(axi...  52.2 us
    ppermute x12, waiting for transfers between devices, sum_blk(): total = total + lax.ppermute(piece, 'blk', pairs).astype(jnp.float32)  28.6 us
    unnamed x181, local copies, waits for them, and re-layouts  27.4 us
    ppermute x12, starting transfers between devices, sum_blk(): total = total + lax.ppermute(piece, 'blk', pairs).astype(jnp.float32)  23 us
    ppermute x4, starting transfers between devices, move(): return lax.ppermute(block, 'blk', pairs)  18.3 us
    gather x6, local copies, waits for them, and re-layouts, in_order(): return jnp.take(jnp.stack(entries), order, axis=0)  11.9 us
  transfers between devices with their start and end apart: 69, of which 31 were waited for; matrix products, arithmetic and copies ran while one was open for 50% of the time, Pallas kernels for 0%

profile of v1, /device:TPU:0, one launch (start us, length us, event | category | flops | bytes accessed | tf_op | source)
XLA Modules:
  0.0 564.2 jit_solution(16620608898838350294)
XLA Ops:
  1.5 2.6 convert_reduce_fusion.2
  4.9 5.7 %collective-permute-start.1 = (bf16[192,1152]{1,0:T(8,128)(2,1)}, bf16[192,1152]{1,0:T(8,128)(2,1)}, u32[]{:S(2)}, u32[]{:S(2)}) collective-permute-start(bf16[192,1152]{1,0:T(8,128)(2,1)} %constant_dynamic-slice_fusion.9), channel_id=1, source_target_pairs={{0,2},{2,4},{4,6},{1,3},{3,5},{5,7},{8,10},{10,12},{12,14},{9,11},... | collective-permute-start | bytes 1327112 | tf_op jit(solution)/shard_map/ppermute | solution.py:53
  12.0 5.6 convolution_add_fusion.3
  35.8 4.3 convert_reduce_fusion.4
  49.1 3.6 fusion.109
  54.3 2.7 copy.74
  57.0 2.4 copy.76
  61.0 27.3 %while.25 = (s32[]{:T(128)}, bf16[8,384,72]{1,2,0:T(8,128)(2,1)S(1)}, pred[768,768]{1,0:T(32,128)(4,1)}, bf16[8,768,72]{2,1,0:T(8,128)(2,1)}, bf16[8,768,72]{2,1...) while((s32[]{:T(128)}, bf16[8,384,72]{1,2,0:T(8,128)(2,1)S(1)}, pred[768,768]{1,0:T(32,128)(4,1)}, ...), condition=%wide.region_8.9_spmd, body=%wide.region_5.8_spmd.sunk | while | flops 87293184 | bytes 4446797 | solution.py:271
  90.7 5.0 fusion.189
  97.3 6.4 %collective-permute-done.18 = bf16[384,640]{1,0:T(8,128)(2,1)S(1)} collective-permute-done((bf16[384,640]{1,0:T(8,128)(2,1)S(1)}, bf16[384,640]{1,0:T(8,128)(2,1)S(1)}, u32[]{:S(2)}, u32[]{:S(2)}) %collective-permute-start.18) | collective-permute-done | bytes 491552 | tf_op jit(solution)/shard_map/ppermute | solution.py:39
  105.0 8.7 %collective-permute-done.58 = bf16[384,640]{1,0:T(8,128)(2,1)S(1)} collective-permute-done((bf16[384,640]{1,0:T(8,128)(2,1)S(1)}, bf16[384,640]{1,0:T(8,128)(2,1)S(1)}, u32[]{:S(2)}, u32[]{:S(2)}) %collective-permute-start.58) | collective-permute-done | bytes 491552 | tf_op jit(solution)/shard_map/ppermute | solution.py:39
  118.9 5.2 convert_reduce_fusion
  125.4 2.4 collective-permute-start.62
  127.8 3.4 convolution_convert_fusion.3
  131.2 3.7 fusion.190
  138.5 9.7 %collective-permute-done.61 = bf16[384,640]{1,0:T(8,128)(2,1)S(1)} collective-permute-done((bf16[384,640]{1,0:T(8,128)(2,1)S(1)}, bf16[384,640]{1,0:T(8,128)(2,1)S(1)}, u32[]{:S(2)}, u32[]{:S(2)}) %collective-permute-start.61) | collective-permute-done | bytes 491552 | tf_op jit(solution)/shard_map/ppermute | solution.py:39
  148.2 3.0 fusion.59
  151.3 2.7 collective-permute-start.63
  154.0 2.6 collective-permute-start.64
  160.6 5.1 collective-permute-done.63
  166.8 12.6 %collective-permute-done.64 = bf16[288,640]{1,0:T(8,128)(2,1)S(1)} collective-permute-done((bf16[288,640]{1,0:T(8,128)(2,1)S(1)}, bf16[288,640]{1,0:T(8,128)(2,1)S(1)}, u32[]{:S(2)}, u32[]{:S(2)}) %collective-permute-start.64) | collective-permute-done | bytes 368672 | tf_op jit(solution)/shard_map/ppermute | solution.py:122
  183.5 7.2 %collective-permute-done.66 = bf16[288,640]{1,0:T(8,128)(2,1)S(1)} collective-permute-done((bf16[288,640]{1,0:T(8,128)(2,1)S(1)}, bf16[288,640]{1,0:T(8,128)(2,1)S(1)}, u32[]{:S(2)}, u32[]{:S(2)}) %collective-permute-start.66) | collective-permute-done | bytes 368672 | tf_op jit(solution)/shard_map/ppermute | solution.py:39
  197.0 6.4 %collective-permute-done.67 = bf16[288,640]{1,0:T(8,128)(2,1)S(1)} collective-permute-done((bf16[288,640]{1,0:T(8,128)(2,1)S(1)}, bf16[288,640]{1,0:T(8,128)(2,1)S(1)}, u32[]{:S(2)}, u32[]{:S(2)}) %collective-permute-start.67) | collective-permute-done | bytes 368672 | tf_op jit(solution)/shard_map/ppermute | solution.py:39
  203.5 7.2 %collective-permute-done.68 = bf16[288,640]{1,0:T(8,128)(2,1)S(1)} collective-permute-done((bf16[288,640]{1,0:T(8,128)(2,1)S(1)}, bf16[288,640]{1,0:T(8,128)(2,1)S(1)}, u32[]{:S(2)}, u32[]{:S(2)}) %collective-permute-start.68) | collective-permute-done | bytes 368672 | tf_op jit(solution)/shard_map/ppermute | solution.py:39
  212.0 3.2 gather_fusion.7
  215.2 3.6 fusion.128
  220.9 5.1 fusion.116
  226.9 9.8 %collective-permute-start.7 = (bf16[384,576]{0,1:T(8,128)(2,1)S(1)}, bf16[384,576]{0,1:T(8,128)(2,1)S(1)}, u32[]{:S(2)}, u32[]{:S(2)}) collective-permute-start(bf16[384,576]{0,1:T(8,128)(2,1)S(1)} %convolution_convert_fusion.5), channel_id=1, source_target_pairs={{0,2},{2,4},{4,6},{1,3},{3,5},{5,7},{8,10},{10,12},{12,14},{9,11},... | collective-permute-start | bytes 1327112 | tf_op jit(solution)/shard_map/ppermute | solution.py:53
  239.9 2.7 fusion.66
  242.6 2.5 collective-permute-done.7
  245.1 4.1 collective-permute-done.8
  252.7 68.0 %while.26 = (s32[]{:T(128)}, bf16[8,384,72]{1,2,0:T(8,128)(2,1)}, bf16[8,384,72]{1,2,0:T(8,128)(2,1)}, bf16[8,384,72]{1,2,0:T(8,128)(2,1)}, bf16[8,768,72]{2,1,0...) while((s32[]{:T(128)}, bf16[8,384,72]{1,2,0:T(8,128)(2,1)}, ...), condition=%wide.region_17.18_spmd.clone, body=%wide.region_13.17_spmd.clone.sunk | while | flops 304992000 | bytes 21209188 | solution.py:319
  326.1 3.2 convolution_convert_fusion.2
  335.4 6.0 %collective-permute-done.23 = bf16[384,432]{0,1:T(8,128)(2,1)S(1)} collective-permute-done((bf16[384,432]{0,1:T(8,128)(2,1)S(1)}, bf16[384,432]{0,1:T(8,128)(2,1)S(1)}, u32[]{:S(2)}, u32[]{:S(2)}) %collective-permute-start.23) | collective-permute-done | bytes 331808 | tf_op jit(solution)/shard_map/ppermute | solution.py:39
  344.5 17.0 %collective-permute-done.30 = bf16[384,640]{1,0:T(8,128)(2,1)S(1)} collective-permute-done((bf16[384,640]{1,0:T(8,128)(2,1)S(1)}, bf16[384,640]{1,0:T(8,128)(2,1)S(1)}, u32[]{:S(2)}, u32[]{:S(2)}) %collective-permute-start.30) | collective-permute-done | bytes 491552 | tf_op jit(solution)/shard_map/ppermute | solution.py:39
  363.4 5.4 collective-permute-done.32
  373.1 3.2 collective-permute-done.25
  376.4 2.4 collective-permute-start.49
  385.1 9.5 %collective-permute-done.48 = bf16[384,640]{1,0:T(8,128)(2,1)S(1)} collective-permute-done((bf16[384,640]{1,0:T(8,128)(2,1)S(1)}, bf16[384,640]{1,0:T(8,128)(2,1)S(1)}, u32[]{:S(2)}, u32[]{:S(2)}) %collective-permute-start.48) | collective-permute-done | bytes 491552 | tf_op jit(solution)/shard_map/ppermute | solution.py:39
  394.6 4.6 fusion.55
  413.5 4.7 reduce_sum.190
  419.4 2.6 dynamic-slice_convert_fusion.5
  425.1 2.9 collective-permute-done.10
  428.0 2.7 fusion.65
  430.6 2.9 collective-permute-start.51
  433.5 10.6 %collective-permute-done.11 = f32[153,128]{1,0:T(8,128)S(1)} collective-permute-done((f32[153,128]{1,0:T(8,128)S(1)}, f32[153,128]{1,0:T(8,128)S(1)}, u32[]{:S(2)}, u32[]{:S(2)}) %collective-permute-start.11) | collective-permute-done | bytes 78368 | tf_op jit(solution)/shard_map/ppermute | solution.py:39
  450.0 4.6 collective-permute-start.52
  462.1 3.1 fusion.126
  465.2 3.4 copy.82
  470.6 2.4 add_convert_fusion.1
  477.1 2.1 bitcast_select_fusion
  481.5 2.7 convolution_add_fusion
  486.7 4.4 convolution_bitcast_fusion.2
  493.2 6.4 %reshape.354 = f32[288,6,576]{2,1,0:T(8,128)} reshape(f32[288,3456]{1,0:T(8,128)} %convolution_add_fusion) | data formatting | bytes 7962624 | tf_op jit(solution)/shard_map/reshape | solution.py:393
  499.7 5.6 copy.84
  508.8 8.9 %collective-permute-done.53 = bf16[288,640]{1,0:T(8,128)(2,1)S(1)} collective-permute-done((bf16[288,640]{1,0:T(8,128)(2,1)}, bf16[288,640]{1,0:T(8,128)(2,1)S(1)}, u32[]{:S(2)}, u32[]{:S(2)}) %collective-permute-start.53) | collective-permute-done | bytes 368672 | tf_op jit(solution)/shard_map/ppermute | solution.py:39
  519.3 6.3 %collective-permute-done.55 = bf16[288,640]{1,0:T(8,128)(2,1)S(1)} collective-permute-done((bf16[288,640]{1,0:T(8,128)(2,1)}, bf16[288,640]{1,0:T(8,128)(2,1)S(1)}, u32[]{:S(2)}, u32[]{:S(2)}) %collective-permute-start.55) | collective-permute-done | bytes 368672 | tf_op jit(solution)/shard_map/ppermute | solution.py:39
  525.5 2.4 pad_maximum_fusion.4
  528.0 3.3 gather_fusion.6
  531.3 2.2 broadcast_select_fusion.4
  540.6 2.2 collective-permute-start.38
  544.5 4.0 collective-permute-done.37
  548.5 3.2 collective-permute-done.38
  554.2 2.5 collective-permute-done.40
  (522 shorter events, 255.6 us)
Async XLA Ops:
  4.9 38.8 %collective-permute-start.1 = (bf16[192,1152]{1,0:T(8,128)(2,1)}, bf16[192,1152]{1,0:T(8,128)(2,1)}, u32[]{:S(2)}, u32[]{:S(2)}) collective-permute-start(bf16[192,1152]{1,0:T(8,128)(2,1)} %constant_dynamic-slice_fusion.9), channel_id=1, source_target_pairs={{0,2},{2,4},{4,6},{1,3},{3,5},{5,7},{8,10},{10,12},{12,14},{9,11},... | collective-permute-start | bytes 1327112 | tf_op jit(solution)/shard_map/ppermute | solution.py:53
  10.7 33.1 %collective-permute-start.2 = (bf16[192,1152]{1,0:T(8,128)(2,1)}, bf16[192,1152]{1,0:T(8,128)(2,1)}, u32[]{:S(2)}, u32[]{:S(2)}) collective-permute-start(bf16[192,1152]{1,0:T(8,128)(2,1)} %constant_dynamic-slice_fusion.9), channel_id=1, source_target_pairs={{2,0},{4,2},{6,4},{3,1},{5,3},{7,5},{10,8},{12,10},{14,12},{11,9},... | collective-permute-start | bytes 1327112 | tf_op jit(solution)/shard_map/ppermute | solution.py:53
  17.6 17.1 %collective-permute-start = (f32[9,6,576]{2,0,1:T(8,128)S(1)}, f32[9,6,576]{2,0,1:T(8,128)S(1)}, u32[]{:S(2)}, u32[]{:S(2)}) collective-permute-start(f32[9,6,576]{2,0,1:T(8,128)S(1)} %convolution_add_fusion.3), channel_id=1, source_target_pairs={{0,1},{1,0},{2,3},{3,2},{4,5},{5,4},{6,7},{7,6},{8,9},{9,8},{10,11... | collective-permute-start | bytes 373256 | tf_op jit(solution)/shard_map/ppermute | solution.py:39
  40.2 55.5 %collective-permute-start.56 = (bf16[384,640]{1,0:T(8,128)(2,1)S(1)}, bf16[384,640]{1,0:T(8,128)(2,1)S(1)}, u32[]{:S(2)}, u32[]{:S(2)}) collective-permute-start(bf16[384,640]{1,0:T(8,128)(2,1)S(1)} %slice_select_fusion.4), channel_id=1, source_target_pairs={{0,8},{8,0},{16,24},{24,16},{1,9},{9,1},{17,25},{25,17},{2,10},{10... | collective-permute-start | bytes 1474568 | tf_op jit(solution)/shard_map/ppermute | solution.py:39
  41.7 63.3 %collective-permute-start.57 = (bf16[384,640]{1,0:T(8,128)(2,1)S(1)}, bf16[384,640]{1,0:T(8,128)(2,1)}, u32[]{:S(2)}, u32[]{:S(2)}) collective-permute-start(bf16[384,640]{1,0:T(8,128)(2,1)S(1)} %slice_select_fusion.4), channel_id=1, source_target_pairs={{0,16},{8,24},{16,0},{24,8},{1,17},{9,25},{17,1},{25,9},{2,18},{10... | collective-permute-start | bytes 1474568 | tf_op jit(solution)/shard_map/ppermute | solution.py:39
  89.3 26.8 %collective-permute-start.4 = (f32[384,1152]{1,0:T(8,128)S(1)}, f32[384,1152]{1,0:T(8,128)S(1)}, u32[]{:S(2)}, u32[]{:S(2)}) collective-permute-start(f32[384,1152]{1,0:T(8,128)S(1)} %fusion.188), channel_id=1, source_target_pairs={{0,1},{1,0},{2,3},{3,2},{4,5},{5,4},{6,7},{7,6},{8,9},{9,8},{10,11... | collective-permute-start | bytes 5308424 | tf_op jit(solution)/shard_map/ppermute | solution.py:39
  89.6 14.1 %collective-permute-start.18 = (bf16[384,640]{1,0:T(8,128)(2,1)S(1)}, bf16[384,640]{1,0:T(8,128)(2,1)S(1)}, u32[]{:S(2)}, u32[]{:S(2)}) collective-permute-start(bf16[384,640]{1,0:T(8,128)(2,1)S(1)} %slice_select_fusion.7), channel_id=1, source_target_pairs={{0,16},{8,24},{16,0},{24,8},{1,17},{9,25},{17,1},{25,9},{2,18},{10... | collective-permute-start | bytes 1474568 | tf_op jit(solution)/shard_map/ppermute | solution.py:39
  90.1 24.8 %collective-permute-start.17 = (bf16[384,640]{1,0:T(8,128)(2,1)S(1)}, bf16[384,640]{1,0:T(8,128)(2,1)S(1)}, u32[]{:S(2)}, u32[]{:S(2)}) collective-permute-start(bf16[384,640]{1,0:T(8,128)(2,1)S(1)} %slice_select_fusion.7), channel_id=1, source_target_pairs={{0,8},{8,0},{16,24},{24,16},{1,9},{9,1},{17,25},{25,17},{2,10},{10... | collective-permute-start | bytes 1474568 | tf_op jit(solution)/shard_map/ppermute | solution.py:39
  95.7 17.9 %collective-permute-start.58 = (bf16[384,640]{1,0:T(8,128)(2,1)S(1)}, bf16[384,640]{1,0:T(8,128)(2,1)S(1)}, u32[]{:S(2)}, u32[]{:S(2)}) collective-permute-start(bf16[384,640]{1,0:T(8,128)(2,1)S(1)} %collective-permute-done.56), channel_id=1, source_target_pairs={{0,16},{8,24},{16,0},{24,8},{1,17},{9,25},{17,1},{25,9},{2,18},{10... | collective-permute-start | bytes 1474568 | tf_op jit(solution)/shard_map/ppermute | solution.py:39
  103.7 12.1 %collective-permute-start.19 = (bf16[384,640]{1,0:T(8,128)(2,1)S(1)}, bf16[384,640]{1,0:T(8,128)(2,1)S(1)}, u32[]{:S(2)}, u32[]{:S(2)}) collective-permute-start(bf16[384,640]{1,0:T(8,128)(2,1)S(1)} %collective-permute-done.18), channel_id=1, source_target_pairs={{0,8},{8,0},{16,24},{24,16},{1,9},{9,1},{17,25},{25,17},{2,10},{10... | collective-permute-start | bytes 1474568 | tf_op jit(solution)/shard_map/ppermute | solution.py:39
  114.9 20.1 %collective-permute-start.59 = (bf16[1536,640]{1,0:T(8,128)(2,1)S(1)}, bf16[1536,640]{1,0:T(8,128)(2,1)S(1)}, u32[]{:S(2)}, u32[]{:S(2)}) collective-permute-start(bf16[1536,640]{1,0:T(8,128)(2,1)S(1)} %pad_maximum_fusion.3), channel_id=1, source_target_pairs={{0,1},{1,0},{2,3},{3,2},{4,5},{5,4},{6,7},{7,6},{8,9},{9,8},{10,11... | collective-permute-start | bytes 5898248 | tf_op jit(solution)/shard_map/ppermute | solution.py:39
  116.0 64.2 %collective-permute-start.20 = (bf16[1536,640]{1,0:T(8,128)(2,1)S(1)}, bf16[1536,640]{1,0:T(8,128)(2,1)S(1)}, u32[]{:S(2)}, u32[]{:S(2)}) collective-permute-start(bf16[1536,640]{1,0:T(8,128)(2,1)S(1)} %pad_maximum_fusion), channel_id=1, source_target_pairs={{0,1},{1,0},{2,3},{3,2},{4,5},{5,4},{6,7},{7,6},{8,9},{9,8},{10,11... | collective-permute-start | bytes 5898248 | tf_op jit(solution)/shard_map/ppermute | solution.py:39
  124.3 14.2 %collective-permute-start.60 = (bf16[384,640]{1,0:T(8,128)(2,1)S(1)}, bf16[384,640]{1,0:T(8,128)(2,1)S(1)}, u32[]{:S(2)}, u32[]{:S(2)}) collective-permute-start(bf16[384,640]{1,0:T(8,128)(2,1)S(1)} %get-tuple-element.264), channel_id=1, source_target_pairs={{0,8},{8,0},{16,24},{24,16},{1,9},{9,1},{17,25},{25,17},{2,10},{10... | collective-permute-start | bytes 1474568 | tf_op jit(solution)/shard_map/ppermute | solution.py:39
  124.9 23.2 %collective-permute-start.61 = (bf16[384,640]{1,0:T(8,128)(2,1)S(1)}, bf16[384,640]{1,0:T(8,128)(2,1)S(1)}, u32[]{:S(2)}, u32[]{:S(2)}) collective-permute-start(bf16[384,640]{1,0:T(8,128)(2,1)S(1)} %get-tuple-element.263), channel_id=1, source_target_pairs={{0,16},{8,24},{16,0},{24,8},{1,17},{9,25},{17,1},{25,9},{2,18},{10... | collective-permute-start | bytes 1474568 | tf_op jit(solution)/shard_map/ppermute | solution.py:39
  125.4 22.8 %collective-permute-start.62 = (bf16[384,640]{1,0:T(8,128)(2,1)S(1)}, bf16[384,640]{1,0:T(8,128)(2,1)S(1)}, u32[]{:S(2)}, u32[]{:S(2)}) collective-permute-start(bf16[384,640]{1,0:T(8,128)(2,1)S(1)} %get-tuple-element.262), channel_id=1, source_target_pairs={{0,24},{8,16},{16,8},{24,0},{1,25},{9,17},{17,9},{25,1},{2,26},{10... | collective-permute-start | bytes 1474568 | tf_op jit(solution)/shard_map/ppermute | solution.py:39
  151.3 14.3 %collective-permute-start.63 = (bf16[288,640]{1,0:T(8,128)(2,1)S(1)}, bf16[288,640]{1,0:T(8,128)(2,1)S(1)}, u32[]{:S(2)}, u32[]{:S(2)}) collective-permute-start(bf16[288,640]{1,0:T(8,128)(2,1)S(1)} %get-tuple-element.246), channel_id=1, source_target_pairs={{0,2},{2,4},{4,6},{6,0},{1,3},{3,5},{5,7},{7,1},{8,10},{10,12},{12... | collective-permute-start | bytes 1105928 | tf_op jit(solution)/shard_map/ppermute | solution.py:122
  154.0 25.4 %collective-permute-start.64 = (bf16[288,640]{1,0:T(8,128)(2,1)S(1)}, bf16[288,640]{1,0:T(8,128)(2,1)S(1)}, u32[]{:S(2)}, u32[]{:S(2)}) collective-permute-start(bf16[288,640]{1,0:T(8,128)(2,1)S(1)} %get-tuple-element.248), channel_id=1, source_target_pairs={{0,4},{2,6},{4,0},{6,2},{1,5},{3,7},{5,1},{7,3},{8,12},{10,14},{12... | collective-permute-start | bytes 1105928 | tf_op jit(solution)/shard_map/ppermute | solution.py:122
  156.6 22.8 %collective-permute-start.65 = (bf16[288,640]{1,0:T(8,128)(2,1)S(1)}, bf16[288,640]{1,0:T(8,128)(2,1)S(1)}, u32[]{:S(2)}, u32[]{:S(2)}) collective-permute-start(bf16[288,640]{1,0:T(8,128)(2,1)S(1)} %get-tuple-element.247), channel_id=1, source_target_pairs={{0,6},{2,0},{4,2},{6,4},{1,7},{3,1},{5,3},{7,5},{8,14},{10,8},{12,... | collective-permute-start | bytes 1105928 | tf_op jit(solution)/shard_map/ppermute | solution.py:122
  157.7 23.8 %collective-permute-start.43 = (bf16[384,640]{1,0:T(8,128)(2,1)S(1)}, bf16[384,640]{1,0:T(8,128)(2,1)S(1)}, u32[]{:S(2)}, u32[]{:S(2)}) collective-permute-start(bf16[384,640]{1,0:T(8,128)(2,1)S(1)} %slice_select_fusion.5), channel_id=1, source_target_pairs={{0,8},{8,0},{16,24},{24,16},{1,9},{9,1},{17,25},{25,17},{2,10},{10... | collective-permute-start | bytes 1474568 | tf_op jit(solution)/shard_map/ppermute | solution.py:39
  165.7 28.2 %collective-permute-start.44 = (bf16[384,640]{1,0:T(8,128)(2,1)S(1)}, bf16[384,640]{1,0:T(8,128)(2,1)S(1)}, u32[]{:S(2)}, u32[]{:S(2)}) collective-permute-start(bf16[384,640]{1,0:T(8,128)(2,1)S(1)} %slice_select_fusion.5), channel_id=1, source_target_pairs={{0,16},{8,24},{16,0},{24,8},{1,17},{9,25},{17,1},{25,9},{2,18},{10... | collective-permute-start | bytes 1474568 | tf_op jit(solution)/shard_map/ppermute | solution.py:39
  179.4 35.8 %collective-permute-start.6 = (f32[384,1152]{1,0:T(8,128)}, f32[384,1152]{1,0:T(8,128)}, u32[]{:S(2)}, u32[]{:S(2)}) collective-permute-start(f32[384,1152]{1,0:T(8,128)} %fusion.190), channel_id=1, source_target_pairs={{0,1},{1,0},{2,3},{3,2},{4,5},{5,4},{6,7},{7,6},{8,9},{9,8},{10,11... | collective-permute-start | bytes 5308424 | tf_op jit(solution)/shard_map/ppermute | solution.py:39
  179.6 11.1 %collective-permute-start.66 = (bf16[288,640]{1,0:T(8,128)(2,1)S(1)}, bf16[288,640]{1,0:T(8,128)(2,1)S(1)}, u32[]{:S(2)}, u32[]{:S(2)}) collective-permute-start(bf16[288,640]{1,0:T(8,128)(2,1)S(1)} %add_convert_fusion), channel_id=1, source_target_pairs={{0,8},{8,0},{16,24},{24,16},{1,9},{9,1},{17,25},{25,17},{2,10},{10... | collective-permute-start | bytes 1105928 | tf_op jit(solution)/shard_map/ppermute | solution.py:39
  181.5 14.1 %collective-permute-start.45 = (bf16[384,640]{1,0:T(8,128)(2,1)S(1)}, bf16[384,640]{1,0:T(8,128)(2,1)S(1)}, u32[]{:S(2)}, u32[]{:S(2)}) collective-permute-start(bf16[384,640]{1,0:T(8,128)(2,1)S(1)} %collective-permute-done.43), channel_id=1, source_target_pairs={{0,16},{8,24},{16,0},{24,8},{1,17},{9,25},{17,1},{25,9},{2,18},{10... | collective-permute-start | bytes 1474568 | tf_op jit(solution)/shard_map/ppermute | solution.py:39
  183.1 20.4 %collective-permute-start.67 = (bf16[288,640]{1,0:T(8,128)(2,1)S(1)}, bf16[288,640]{1,0:T(8,128)(2,1)S(1)}, u32[]{:S(2)}, u32[]{:S(2)}) collective-permute-start(bf16[288,640]{1,0:T(8,128)(2,1)S(1)} %add_convert_fusion), channel_id=1, source_target_pairs={{0,16},{8,24},{16,0},{24,8},{1,17},{9,25},{17,1},{25,9},{2,18},{10... | collective-permute-start | bytes 1105928 | tf_op jit(solution)/shard_map/ppermute | solution.py:39
  190.7 20.0 %collective-permute-start.68 = (bf16[288,640]{1,0:T(8,128)(2,1)S(1)}, bf16[288,640]{1,0:T(8,128)(2,1)S(1)}, u32[]{:S(2)}, u32[]{:S(2)}) collective-permute-start(bf16[288,640]{1,0:T(8,128)(2,1)S(1)} %collective-permute-done.66), channel_id=1, source_target_pairs={{0,16},{8,24},{16,0},{24,8},{1,17},{9,25},{17,1},{25,9},{2,18},{10... | collective-permute-start | bytes 1105928 | tf_op jit(solution)/shard_map/ppermute | solution.py:39
  193.9 25.5 %collective-permute-start.5 = (bf16[384,1152]{1,0:T(8,128)(2,1)}, bf16[384,1152]{1,0:T(8,128)(2,1)}, u32[]{:S(2)}, u32[]{:S(2)}) collective-permute-start(bf16[384,1152]{1,0:T(8,128)(2,1)} %convolution_convert_fusion.3), channel_id=1, source_target_pairs={{0,1},{1,0},{2,3},{3,2},{4,5},{5,4},{6,7},{7,6},{8,9},{9,8},{10,11... | collective-permute-start | bytes 2654216 | tf_op jit(solution)/shard_map/ppermute | solution.py:39
  197.0 182.5 %collective-permute-start.46 = (bf16[1536,640]{1,0:T(8,128)(2,1)}, bf16[1536,640]{1,0:T(8,128)(2,1)}, u32[]{:S(2)}, u32[]{:S(2)}) collective-permute-start(bf16[1536,640]{1,0:T(8,128)(2,1)} %pad_maximum_fusion.2), channel_id=1, source_target_pairs={{0,1},{1,0},{2,3},{3,2},{4,5},{5,4},{6,7},{7,6},{8,9},{9,8},{10,11... | collective-permute-start | bytes 5898248 | tf_op jit(solution)/shard_map/ppermute | solution.py:39
  226.9 18.2 %collective-permute-start.7 = (bf16[384,576]{0,1:T(8,128)(2,1)S(1)}, bf16[384,576]{0,1:T(8,128)(2,1)S(1)}, u32[]{:S(2)}, u32[]{:S(2)}) collective-permute-start(bf16[384,576]{0,1:T(8,128)(2,1)S(1)} %convolution_convert_fusion.5), channel_id=1, source_target_pairs={{0,2},{2,4},{4,6},{1,3},{3,5},{5,7},{8,10},{10,12},{12,14},{9,11},... | collective-permute-start | bytes 1327112 | tf_op jit(solution)/shard_map/ppermute | solution.py:53
  236.7 12.5 %collective-permute-start.8 = (bf16[384,576]{0,1:T(8,128)(2,1)S(1)}, bf16[384,576]{0,1:T(8,128)(2,1)S(1)}, u32[]{:S(2)}, u32[]{:S(2)}) collective-permute-start(bf16[384,576]{0,1:T(8,128)(2,1)S(1)} %convolution_convert_fusion.5), channel_id=1, source_target_pairs={{2,0},{4,2},{6,4},{3,1},{5,3},{7,5},{10,8},{12,10},{14,12},{11,9},... | collective-permute-start | bytes 1327112 | tf_op jit(solution)/shard_map/ppermute | solution.py:53
  238.3 92.4 %collective-permute-start.31 = (bf16[384,640]{1,0:T(8,128)(2,1)S(1)}, bf16[384,640]{1,0:T(8,128)(2,1)}, u32[]{:S(2)}, u32[]{:S(2)}) collective-permute-start(bf16[384,640]{1,0:T(8,128)(2,1)S(1)} %slice_select_fusion.6), channel_id=1, source_target_pairs={{0,16},{8,24},{16,0},{24,8},{1,17},{9,25},{17,1},{25,9},{2,18},{10... | collective-permute-start | bytes 1474568 | tf_op jit(solution)/shard_map/ppermute | solution.py:39
  322.5 10.8 %collective-permute-start.21 = (bf16[384,432]{0,1:T(8,128)(2,1)S(1)}, bf16[384,432]{0,1:T(8,128)(2,1)S(1)}, u32[]{:S(2)}, u32[]{:S(2)}) collective-permute-start(bf16[384,432]{0,1:T(8,128)(2,1)S(1)} %get-tuple-element.283), channel_id=1, source_target_pairs={{0,8},{8,0},{16,24},{24,16},{1,9},{9,1},{17,25},{25,17},{2,10},{10... | collective-permute-start | bytes 995336 | tf_op jit(solution)/shard_map/ppermute | solution.py:39
  324.1 11.3 %collective-permute-start.22 = (bf16[384,432]{0,1:T(8,128)(2,1)S(1)}, bf16[384,432]{0,1:T(8,128)(2,1)S(1)}, u32[]{:S(2)}, u32[]{:S(2)}) collective-permute-start(bf16[384,432]{0,1:T(8,128)(2,1)S(1)} %get-tuple-element.282), channel_id=1, source_target_pairs={{0,16},{8,24},{16,0},{24,8},{1,17},{9,25},{17,1},{25,9},{2,18},{10... | collective-permute-start | bytes 995336 | tf_op jit(solution)/shard_map/ppermute | solution.py:39
  325.6 15.8 %collective-permute-start.23 = (bf16[384,432]{0,1:T(8,128)(2,1)S(1)}, bf16[384,432]{0,1:T(8,128)(2,1)S(1)}, u32[]{:S(2)}, u32[]{:S(2)}) collective-permute-start(bf16[384,432]{0,1:T(8,128)(2,1)S(1)} %get-tuple-element.281), channel_id=1, source_target_pairs={{0,24},{8,16},{16,8},{24,0},{1,25},{9,17},{17,9},{25,1},{2,26},{10... | collective-permute-start | bytes 995336 | tf_op jit(solution)/shard_map/ppermute | solution.py:39
  330.7 53.0 %collective-permute-start.47 = (bf16[384,640]{1,0:T(8,128)(2,1)S(1)}, bf16[384,640]{1,0:T(8,128)(2,1)S(1)}, u32[]{:S(2)}, u32[]{:S(2)}) collective-permute-start(bf16[384,640]{1,0:T(8,128)(2,1)S(1)} %copy-done.49), channel_id=1, source_target_pairs={{0,8},{8,0},{16,24},{24,16},{1,9},{9,1},{17,25},{25,17},{2,10},{10... | collective-permute-start | bytes 1474568 | tf_op jit(solution)/shard_map/ppermute | solution.py:39
  333.3 28.2 %collective-permute-start.30 = (bf16[384,640]{1,0:T(8,128)(2,1)S(1)}, bf16[384,640]{1,0:T(8,128)(2,1)S(1)}, u32[]{:S(2)}, u32[]{:S(2)}) collective-permute-start(bf16[384,640]{1,0:T(8,128)(2,1)S(1)} %slice_select_fusion.6), channel_id=1, source_target_pairs={{0,8},{8,0},{16,24},{24,16},{1,9},{9,1},{17,25},{25,17},{2,10},{10... | collective-permute-start | bytes 1474568 | tf_op jit(solution)/shard_map/ppermute | solution.py:39
  335.4 33.4 %collective-permute-start.32 = (bf16[384,640]{1,0:T(8,128)(2,1)}, bf16[384,640]{1,0:T(8,128)(2,1)S(1)}, u32[]{:S(2)}, u32[]{:S(2)}) collective-permute-start(bf16[384,640]{1,0:T(8,128)(2,1)} %collective-permute-done.31), channel_id=1, source_target_pairs={{0,8},{8,0},{16,24},{24,16},{1,9},{9,1},{17,25},{25,17},{2,10},{10... | collective-permute-start | bytes 1474568 | tf_op jit(solution)/shard_map/ppermute | solution.py:39
  343.7 27.8 %collective-permute-start.24 = (bf16[288,432]{0,1:T(8,128)(2,1)S(1)}, bf16[288,432]{0,1:T(8,128)(2,1)S(1)}, u32[]{:S(2)}, u32[]{:S(2)}) collective-permute-start(bf16[288,432]{0,1:T(8,128)(2,1)S(1)} %get-tuple-element.253), channel_id=1, source_target_pairs={{0,2},{2,4},{4,6},{6,0},{1,3},{3,5},{5,7},{7,1},{8,10},{10,12},{12... | collective-permute-start | bytes 746504 | tf_op jit(solution)/shard_map/ppermute | solution.py:122
  361.5 14.9 %collective-permute-start.25 = (bf16[288,432]{0,1:T(8,128)(2,1)S(1)}, bf16[288,432]{0,1:T(8,128)(2,1)S(1)}, u32[]{:S(2)}, u32[]{:S(2)}) collective-permute-start(bf16[288,432]{0,1:T(8,128)(2,1)S(1)} %get-tuple-element.255), channel_id=1, source_target_pairs={{0,4},{2,6},{4,0},{6,2},{1,5},{3,7},{5,1},{7,3},{8,12},{10,14},{12... | collective-permute-start | bytes 746504 | tf_op jit(solution)/shard_map/ppermute | solution.py:122
  368.8 10.5 %collective-permute-start.26 = (bf16[288,432]{0,1:T(8,128)(2,1)S(1)}, bf16[288,432]{0,1:T(8,128)(2,1)S(1)}, u32[]{:S(2)}, u32[]{:S(2)}) collective-permute-start(bf16[288,432]{0,1:T(8,128)(2,1)S(1)} %get-tuple-element.254), channel_id=1, source_target_pairs={{0,6},{2,0},{4,2},{6,4},{1,7},{3,1},{5,3},{7,5},{8,14},{10,8},{12,... | collective-permute-start | bytes 746504 | tf_op jit(solution)/shard_map/ppermute | solution.py:122
  371.5 23.1 %collective-permute-start.48 = (bf16[384,640]{1,0:T(8,128)(2,1)S(1)}, bf16[384,640]{1,0:T(8,128)(2,1)S(1)}, u32[]{:S(2)}, u32[]{:S(2)}) collective-permute-start(bf16[384,640]{1,0:T(8,128)(2,1)S(1)} %copy-done.48), channel_id=1, source_target_pairs={{0,16},{8,24},{16,0},{24,8},{1,17},{9,25},{17,1},{25,9},{2,18},{10... | collective-permute-start | bytes 1474568 | tf_op jit(solution)/shard_map/ppermute | solution.py:39
  376.4 18.2 %collective-permute-start.49 = (bf16[384,640]{1,0:T(8,128)(2,1)S(1)}, bf16[384,640]{1,0:T(8,128)(2,1)S(1)}, u32[]{:S(2)}, u32[]{:S(2)}) collective-permute-start(bf16[384,640]{1,0:T(8,128)(2,1)S(1)} %copy-done.47), channel_id=1, source_target_pairs={{0,24},{8,16},{16,8},{24,0},{1,25},{9,17},{17,9},{25,1},{2,26},{10... | collective-permute-start | bytes 1474568 | tf_op jit(solution)/shard_map/ppermute | solution.py:39
  379.2 20.0 %collective-permute-start.9 = (bf16[384,1152]{1,0:T(8,128)(2,1)S(1)}, bf16[384,1152]{1,0:T(8,128)(2,1)S(1)}, u32[]{:S(2)}, u32[]{:S(2)}) collective-permute-start(bf16[384,1152]{1,0:T(8,128)(2,1)S(1)} %convolution_convert_fusion.2), channel_id=1, source_target_pairs={{0,1},{1,0},{2,3},{3,2},{4,5},{5,4},{6,7},{7,6},{8,9},{9,8},{10,11... | collective-permute-start | bytes 2654216 | tf_op jit(solution)/shard_map/ppermute | solution.py:39
  379.6 51.1 %collective-permute-start.28 = (bf16[288,432]{0,1:T(8,128)(2,1)S(1)}, bf16[288,432]{0,1:T(8,128)(2,1)}, u32[]{:S(2)}, u32[]{:S(2)}) collective-permute-start(bf16[288,432]{0,1:T(8,128)(2,1)S(1)} %add_convert_fusion.2), channel_id=1, source_target_pairs={{0,16},{8,24},{16,0},{24,8},{1,17},{9,25},{17,1},{25,9},{2,18},{10... | collective-permute-start | bytes 746504 | tf_op jit(solution)/shard_map/ppermute | solution.py:39
  383.7 66.3 %collective-permute-start.27 = (bf16[288,432]{0,1:T(8,128)(2,1)S(1)}, bf16[288,432]{0,1:T(8,128)(2,1)}, u32[]{:S(2)}, u32[]{:S(2)}) collective-permute-start(bf16[288,432]{0,1:T(8,128)(2,1)S(1)} %add_convert_fusion.2), channel_id=1, source_target_pairs={{0,8},{8,0},{16,24},{24,16},{1,9},{9,1},{17,25},{25,17},{2,10},{10... | collective-permute-start | bytes 746504 | tf_op jit(solution)/shard_map/ppermute | solution.py:39
  418.6 9.3 %collective-permute-start.10 = (f32[153,128]{1,0:T(8,128)S(1)}, f32[153,128]{1,0:T(8,128)S(1)}, u32[]{:S(2)}, u32[]{:S(2)}) collective-permute-start(f32[153,128]{1,0:T(8,128)S(1)} %bitcast.387), channel_id=1, source_target_pairs={{0,2},{2,0},{4,6},{6,4},{1,3},{3,1},{5,7},{7,5},{8,10},{10,8},{12,... | collective-permute-start | bytes 235016 | tf_op jit(solution)/shard_map/ppermute | solution.py:39
  422.1 46.5 %collective-permute-start.50 = (bf16[288,640]{1,0:T(8,128)(2,1)}, bf16[288,640]{1,0:T(8,128)(2,1)}, u32[]{:S(2)}, u32[]{:S(2)}) collective-permute-start(bf16[288,640]{1,0:T(8,128)(2,1)} %get-tuple-element.249), channel_id=1, source_target_pairs={{0,2},{2,4},{4,6},{6,0},{1,3},{3,5},{5,7},{7,1},{8,10},{10,12},{12... | collective-permute-start | bytes 1105928 | tf_op jit(solution)/shard_map/ppermute | solution.py:122
  423.3 20.9 %collective-permute-start.11 = (f32[153,128]{1,0:T(8,128)S(1)}, f32[153,128]{1,0:T(8,128)S(1)}, u32[]{:S(2)}, u32[]{:S(2)}) collective-permute-start(f32[153,128]{1,0:T(8,128)S(1)} %bitcast.388), channel_id=1, source_target_pairs={{0,4},{2,6},{4,0},{6,2},{1,5},{3,7},{5,1},{7,3},{8,12},{10,14},{12... | collective-permute-start | bytes 235016 | tf_op jit(solution)/shard_map/ppermute | solution.py:39
  427.9 18.0 %collective-permute-start.12 = (f32[153,128]{1,0:T(8,128)S(1)}, f32[153,128]{1,0:T(8,128)S(1)}, u32[]{:S(2)}, u32[]{:S(2)}) collective-permute-start(f32[153,128]{1,0:T(8,128)S(1)} %collective-permute-done.10), channel_id=1, source_target_pairs={{0,4},{2,6},{4,0},{6,2},{1,5},{3,7},{5,1},{7,3},{8,12},{10,14},{12... | collective-permute-start | bytes 235016 | tf_op jit(solution)/shard_map/ppermute | solution.py:39
  430.6 38.2 %collective-permute-start.51 = (bf16[288,640]{1,0:T(8,128)(2,1)}, bf16[288,640]{1,0:T(8,128)(2,1)}, u32[]{:S(2)}, u32[]{:S(2)}) collective-permute-start(bf16[288,640]{1,0:T(8,128)(2,1)} %get-tuple-element.251), channel_id=1, source_target_pairs={{0,4},{2,6},{4,0},{6,2},{1,5},{3,7},{5,1},{7,3},{8,12},{10,14},{12... | collective-permute-start | bytes 1105928 | tf_op jit(solution)/shard_map/ppermute | solution.py:122
  444.2 10.9 %collective-permute-start.29 = (bf16[288,432]{0,1:T(8,128)(2,1)}, bf16[288,432]{0,1:T(8,128)(2,1)}, u32[]{:S(2)}, u32[]{:S(2)}) collective-permute-start(bf16[288,432]{0,1:T(8,128)(2,1)} %collective-permute-done.28), channel_id=1, source_target_pairs={{0,8},{8,0},{16,24},{24,16},{1,9},{9,1},{17,25},{25,17},{2,10},{10... | collective-permute-start | bytes 746504 | tf_op jit(solution)/shard_map/ppermute | solution.py:39
  447.5 13.1 %collective-permute-start.13 = (f32[4,153,128]{2,1,0:T(8,128)}, f32[4,153,128]{2,1,0:T(8,128)}, u32[]{:S(2)}, u32[]{:S(2)}) collective-permute-start(f32[4,153,128]{2,1,0:T(8,128)} %broadcast_select_fusion.8), channel_id=1, source_target_pairs={{0,8},{8,0},{16,24},{24,16},{1,9},{9,1},{17,25},{25,17},{2,10},{10... | collective-permute-start | bytes 940040 | tf_op jit(solution)/shard_map/ppermute | solution.py:39
  450.0 20.6 %collective-permute-start.52 = (bf16[288,640]{1,0:T(8,128)(2,1)}, bf16[288,640]{1,0:T(8,128)(2,1)}, u32[]{:S(2)}, u32[]{:S(2)}) collective-permute-start(bf16[288,640]{1,0:T(8,128)(2,1)} %get-tuple-element.250), channel_id=1, source_target_pairs={{0,6},{2,0},{4,2},{6,4},{1,7},{3,1},{5,3},{7,5},{8,14},{10,8},{12,... | collective-permute-start | bytes 1105928 | tf_op jit(solution)/shard_map/ppermute | solution.py:122
  455.0 18.0 %collective-permute-start.14 = (f32[4,153,128]{2,1,0:T(8,128)}, f32[4,153,128]{2,1,0:T(8,128)}, u32[]{:S(2)}, u32[]{:S(2)}) collective-permute-start(f32[4,153,128]{2,1,0:T(8,128)} %broadcast_select_fusion.8), channel_id=1, source_target_pairs={{0,16},{8,24},{16,0},{24,8},{1,17},{9,25},{17,1},{25,9},{2,18},{10... | collective-permute-start | bytes 940040 | tf_op jit(solution)/shard_map/ppermute | solution.py:39
  460.5 12.8 %collective-permute-start.15 = (f32[4,153,128]{2,1,0:T(8,128)}, f32[4,153,128]{2,1,0:T(8,128)S(1)}, u32[]{:S(2)}, u32[]{:S(2)}) collective-permute-start(f32[4,153,128]{2,1,0:T(8,128)} %collective-permute-done.13), channel_id=1, source_target_pairs={{0,16},{8,24},{16,0},{24,8},{1,17},{9,25},{17,1},{25,9},{2,18},{10... | collective-permute-start | bytes 940040 | tf_op jit(solution)/shard_map/ppermute | solution.py:39
  468.6 70.0 %collective-permute-start.34 = (bf16[384,144]{0,1:T(8,128)(2,1)}, bf16[384,144]{0,1:T(8,128)(2,1)}, u32[]{:S(2)}, u32[]{:S(2)}) collective-permute-start(bf16[384,144]{0,1:T(8,128)(2,1)} %get-tuple-element.294), channel_id=1, source_target_pairs={{0,8},{8,0},{16,24},{24,16},{1,9},{9,1},{17,25},{25,17},{2,10},{10... | collective-permute-start | bytes 331784 | tf_op jit(solution)/shard_map/ppermute | solution.py:39
  468.9 69.8 %collective-permute-start.35 = (bf16[384,144]{0,1:T(8,128)(2,1)}, bf16[384,144]{0,1:T(8,128)(2,1)}, u32[]{:S(2)}, u32[]{:S(2)}) collective-permute-start(bf16[384,144]{0,1:T(8,128)(2,1)} %get-tuple-element.293), channel_id=1, source_target_pairs={{0,16},{8,24},{16,0},{24,8},{1,17},{9,25},{17,1},{25,9},{2,18},{10... | collective-permute-start | bytes 331784 | tf_op jit(solution)/shard_map/ppermute | solution.py:39
  470.6 64.7 %collective-permute-start.33 = (bf16[1536,640]{1,0:T(8,128)(2,1)S(1)}, bf16[1536,640]{1,0:T(8,128)(2,1)}, u32[]{:S(2)}, u32[]{:S(2)}) collective-permute-start(bf16[1536,640]{1,0:T(8,128)(2,1)S(1)} %pad_maximum_fusion.1), channel_id=1, source_target_pairs={{0,1},{1,0},{2,3},{3,2},{4,5},{5,4},{6,7},{7,6},{8,9},{9,8},{10,11... | collective-permute-start | bytes 5898248 | tf_op jit(solution)/shard_map/ppermute | solution.py:39
  473.0 33.0 %collective-permute-start.54 = (bf16[288,640]{1,0:T(8,128)(2,1)}, bf16[288,640]{1,0:T(8,128)(2,1)}, u32[]{:S(2)}, u32[]{:S(2)}) collective-permute-start(bf16[288,640]{1,0:T(8,128)(2,1)} %add_convert_fusion.1), channel_id=1, source_target_pairs={{0,16},{8,24},{16,0},{24,8},{1,17},{9,25},{17,1},{25,9},{2,18},{10... | collective-permute-start | bytes 1105928 | tf_op jit(solution)/shard_map/ppermute | solution.py:39
  491.2 16.6 %collective-permute-start.16 = (f32[9,1152]{1,0:T(8,128)S(1)}, f32[9,1152]{1,0:T(8,128)S(1)}, u32[]{:S(2)}, u32[]{:S(2)}) collective-permute-start(f32[9,1152]{1,0:T(8,128)S(1)} %slice_add_fusion.2), channel_id=1, source_target_pairs={{0,1},{1,0},{2,3},{3,2},{4,5},{5,4},{6,7},{7,6},{8,9},{9,8},{10,11... | collective-permute-start | bytes 124424 | tf_op jit(solution)/shard_map/ppermute | solution.py:39
  506.0 11.6 %collective-permute-start.53 = (bf16[288,640]{1,0:T(8,128)(2,1)}, bf16[288,640]{1,0:T(8,128)(2,1)S(1)}, u32[]{:S(2)}, u32[]{:S(2)}) collective-permute-start(bf16[288,640]{1,0:T(8,128)(2,1)} %add_convert_fusion.1), channel_id=1, source_target_pairs={{0,8},{8,0},{16,24},{24,16},{1,9},{9,1},{17,25},{25,17},{2,10},{10... | collective-permute-start | bytes 1105928 | tf_op jit(solution)/shard_map/ppermute | solution.py:39
  507.8 17.8 %collective-permute-start.55 = (bf16[288,640]{1,0:T(8,128)(2,1)}, bf16[288,640]{1,0:T(8,128)(2,1)S(1)}, u32[]{:S(2)}, u32[]{:S(2)}) collective-permute-start(bf16[288,640]{1,0:T(8,128)(2,1)} %collective-permute-done.54), channel_id=1, source_target_pairs={{0,8},{8,0},{16,24},{24,16},{1,9},{9,1},{17,25},{25,17},{2,10},{10... | collective-permute-start | bytes 1105928 | tf_op jit(solution)/shard_map/ppermute | solution.py:39
  517.6 21.0 %collective-permute-start.36 = (bf16[384,144]{0,1:T(8,128)(2,1)S(1)}, bf16[384,144]{0,1:T(8,128)(2,1)S(1)}, u32[]{:S(2)}, u32[]{:S(2)}) collective-permute-start(bf16[384,144]{0,1:T(8,128)(2,1)S(1)} %get-tuple-element.292), channel_id=1, source_target_pairs={{0,24},{8,16},{16,8},{24,0},{1,25},{9,17},{17,9},{25,1},{2,26},{10... | collective-permute-start | bytes 331784 | tf_op jit(solution)/shard_map/ppermute | solution.py:39
  540.6 11.1 %collective-permute-start.38 = (bf16[288,144]{0,1:T(8,128)(2,1)S(1)}, bf16[288,144]{0,1:T(8,128)(2,1)S(1)}, u32[]{:S(2)}, u32[]{:S(2)}) collective-permute-start(bf16[288,144]{0,1:T(8,128)(2,1)S(1)} %get-tuple-element.288), channel_id=1, source_target_pairs={{0,4},{2,6},{4,0},{6,2},{1,5},{3,7},{5,1},{7,3},{8,12},{10,14},{12... | collective-permute-start | bytes 248840 | tf_op jit(solution)/shard_map/ppermute | solution.py:122
  542.8 8.9 %collective-permute-start.39 = (bf16[288,144]{0,1:T(8,128)(2,1)S(1)}, bf16[288,144]{0,1:T(8,128)(2,1)S(1)}, u32[]{:S(2)}, u32[]{:S(2)}) collective-permute-start(bf16[288,144]{0,1:T(8,128)(2,1)S(1)} %get-tuple-element.287), channel_id=1, source_target_pairs={{0,6},{2,0},{4,2},{6,4},{1,7},{3,1},{5,3},{7,5},{8,14},{10,8},{12,... | collective-permute-start | bytes 248840 | tf_op jit(solution)/shard_map/ppermute | solution.py:122
  (89 other events, 1509.3 us)
